TPU v7x, 512 devices: a whole 4x4x16 slice. The times are simulated.
512 devices in a mesh: dp: 32 (over z, core), ctx: 16 (over x, y).
Axes of the slice: x: 4, y: 4, z: 16, core: 2. Of those that a mesh axis runs over, the one named last changes fastest.
Arguments:
- queries: bfloat16 [65536, 1024], P(('dp', 'ctx')), may hold values from -6 to 6
- key_vectors: bfloat16 [65536, 1024], P(('dp', 'ctx')), may hold values from -6 to 6
- value_vectors: bfloat16 [65536, 1024], P(('dp', 'ctx')), may hold values from -6 to 6
- gate_values: bfloat16 [65536, 1024], P(('dp', 'ctx')), may hold values from -6 to 6
- cotangent: bfloat16 [65536, 1024], P(('dp', 'ctx')), may hold values from -6 to 6
- norm_gain: float32 [1024], replicated, may hold values from 0.5 to 1.5
- lengths: int32 [32, 4], P('dp'), may hold values from 1 to 1024, 2048 in all within a row
Outputs:
- output: bfloat16 [65536, 1024], P(('dp', 'ctx'))
- grad_queries: bfloat16 [65536, 1024], P(('dp', 'ctx'))
- grad_keys: bfloat16 [65536, 1024], P(('dp', 'ctx'))
- grad_values: bfloat16 [65536, 1024], P(('dp', 'ctx'))
- grad_gain: float32 [1024], replicated
Inputs may be any that keep to these rules, and one draw needn't show every extreme that they name: Each group's lengths sum to 2048, and the longest is exactly half of that.
All inputs are finite; a program needn't handle non-finite values.
Results may differ from a plain program's by a relative error of at most 0.0058.
Values may be sent and summed in bfloat16 or wider, within the bound.
A program may use at most 128 MiB of HBM per device.

v0:
```python
import math

import jax
import jax.numpy as jnp
from jax import lax
from jax.sharding import PartitionSpec as P

HEAD = 128


EPSILON = 1e-05


def event_time(rows, row_count, shard_count):
    half = row_count // 2
    shard = rows // row_count
    local = rows % row_count
    early = shard * half + local
    late = (2 * shard_count - 1 - shard) * half + local - half
    return jnp.where(local < half, early, late)


def user_index(positions, user_ends):
    return jnp.sum((positions[:, None] >= user_ends[None, :]).astype(jnp.int32), axis=1)


def pair_mask(query_pos, key_pos, user_ends):
    same = user_index(query_pos, user_ends)[:, None] == user_index(key_pos, user_ends)[None, :]
    before = key_pos[None, :] <= query_pos[:, None]
    return jnp.where(same & before, 1.0, 0.0).astype(jnp.float32)


def head_split(matrix):
    return matrix.reshape(matrix.shape[0], -1, HEAD)


def head_scores(left, right):
    return jnp.einsum(
        "rhd,chd->hrc", head_split(left), head_split(right), preferred_element_type=jnp.float32
    ) / math.sqrt(HEAD)


def silu_slope(scores):
    sigmoid = jax.nn.sigmoid(scores)
    return sigmoid * (1.0 + scores * (1.0 - sigmoid))


def fold_shards(folder, initial, arrays, row_count, shard_count):

    def fold_step(turn_index, carried):
        offset = (turn_index * row_count).astype(jnp.int32)
        pieces = tuple((lax.dynamic_slice_in_dim(array, offset, row_count, 0) for array in arrays))
        return folder(carried, pieces, offset)

    return lax.fori_loop(0, shard_count, fold_step, initial)


def keep_carry(carried):
    return carried


def body(queries, key_vectors, value_vectors, gate_values, cotangent, norm_gain, lengths):
    row_count, width_count = queries.shape
    shard_count = lax.axis_size("ctx")
    first_row = lax.axis_index("ctx") * row_count
    query_pos = event_time(
        first_row + jnp.arange(row_count, dtype=jnp.int32), row_count, shard_count
    )
    user_ends = jnp.cumsum(lengths[0])
    blank_rows = jnp.zeros((row_count, width_count), jnp.float32)

    def forward_fold(running, pieces, offset):
        key_part, value_part = pieces
        piece_rows = key_part.shape[0]
        key_pos = event_time(
            offset + jnp.arange(piece_rows, dtype=jnp.int32), row_count, shard_count
        )
        live = pair_mask(query_pos, key_pos, user_ends)

        def forward_work(carried):
            scores = head_scores(queries, key_part)
            weights = (jax.nn.silu(scores) * live[None]).astype(jnp.bfloat16)
            result = jnp.einsum(
                "hrc,chd->rhd", weights, head_split(value_part), preferred_element_type=jnp.float32
            )
            return carried + result.reshape(carried.shape)

        return lax.cond(jnp.any(live > 0.0), forward_work, keep_carry, running)

    gathered = (
        lax.all_gather(key_vectors, "ctx", axis=0, tiled=True),
        lax.all_gather(value_vectors, "ctx", axis=0, tiled=True),
    )
    attended = fold_shards(forward_fold, blank_rows, gathered, row_count, shard_count)
    row_mean = jnp.mean(attended, axis=1, keepdims=True)
    centered = attended - row_mean
    variance = jnp.mean(centered * centered, axis=1, keepdims=True)
    inverse = lax.rsqrt(variance + EPSILON)
    normed = centered * inverse
    gates = gate_values.astype(jnp.float32)
    grads = cotangent.astype(jnp.float32)
    scaled_gates = gates * norm_gain[None, :]
    output = (normed * scaled_gates).astype(jnp.bfloat16)
    grad_gain = lax.psum(jnp.sum(normed * grads * gates, axis=0), ("dp", "ctx"))
    grad_norm = grads * scaled_gates
    grad_attended = (
        (
            grad_norm
            - jnp.mean(grad_norm, axis=1, keepdims=True)
            - normed * jnp.mean(grad_norm * normed, axis=1, keepdims=True)
        )
        * inverse
    ).astype(jnp.bfloat16)

    def query_fold(running, pieces, offset):
        key_part, value_part = pieces
        piece_rows = key_part.shape[0]
        key_pos = event_time(
            offset + jnp.arange(piece_rows, dtype=jnp.int32), row_count, shard_count
        )
        live = pair_mask(query_pos, key_pos, user_ends)

        def query_work(carried):
            scores = head_scores(queries, key_part)
            grad_weights = jnp.einsum(
                "rhd,chd->hrc",
                head_split(grad_attended),
                head_split(value_part),
                preferred_element_type=jnp.float32,
            )
            grad_scores = (grad_weights * silu_slope(scores) * live[None] / math.sqrt(HEAD)).astype(
                jnp.bfloat16
            )
            result = jnp.einsum(
                "hrc,chd->rhd",
                grad_scores,
                head_split(key_part),
                preferred_element_type=jnp.float32,
            )
            return carried + result.reshape(carried.shape)

        return lax.cond(jnp.any(live > 0.0), query_work, keep_carry, running)

    grad_q_sum = fold_shards(query_fold, blank_rows, gathered, row_count, shard_count)
    query_part = lax.all_gather(queries, "ctx", axis=0, tiled=True)
    grad_part = lax.all_gather(grad_attended, "ctx", axis=0, tiled=True)
    piece_rows = query_part.shape[0]
    other_pos = event_time(jnp.arange(piece_rows, dtype=jnp.int32), row_count, shard_count)
    live = pair_mask(other_pos, query_pos, user_ends)

    def key_work(carried):
        grad_key_sum, grad_value_sum = carried
        scores = head_scores(query_part, key_vectors)
        weights = (jax.nn.silu(scores) * live[None]).astype(jnp.bfloat16)
        grad_weights = jnp.einsum(
            "rhd,chd->hrc",
            head_split(grad_part),
            head_split(value_vectors),
            preferred_element_type=jnp.float32,
        )
        grad_scores = (grad_weights * silu_slope(scores) * live[None] / math.sqrt(HEAD)).astype(
            jnp.bfloat16
        )
        grad_value = jnp.einsum(
            "hrc,rhd->chd", weights, head_split(grad_part), preferred_element_type=jnp.float32
        )
        grad_key = jnp.einsum(
            "hrc,rhd->chd", grad_scores, head_split(query_part), preferred_element_type=jnp.float32
        )
        return (grad_key.reshape(grad_key_sum.shape), grad_value.reshape(grad_value_sum.shape))

    grad_k_sum, grad_v_sum = lax.cond(
        jnp.any(live > 0.0), key_work, keep_carry, (blank_rows, blank_rows)
    )
    return (
        output,
        grad_q_sum.astype(jnp.bfloat16),
        grad_k_sum.astype(jnp.bfloat16),
        grad_v_sum.astype(jnp.bfloat16),
        grad_gain,
    )


def solution(mesh):
    placed = (
        P(("dp", "ctx"), None),
        P(("dp", "ctx"), None),
        P(("dp", "ctx"), None),
        P(("dp", "ctx"), None),
        P(("dp", "ctx"), None),
        P(),
        P("dp", None),
    )
    return jax.shard_map(
        body,
        mesh=mesh,
        in_specs=placed,
        out_specs=(
            P(("dp", "ctx"), None),
            P(("dp", "ctx"), None),
            P(("dp", "ctx"), None),
            P(("dp", "ctx"), None),
            P(),
        ),
        check_vma=False,
    )
```

profile of v0, /device:TPU:6, one launch (start us, length us, event | category | flops | bytes accessed | tf_op | source)
XLA Modules:
  0.0 471.9 jit_solution(17669793501879435348)
XLA Ops:
  7.2 1.8 copy.79
  9.1 1.8 copy.80
  10.9 1.8 copy.83
  16.5 72.1 %all-gather.5.cloned.1.call-done = bf16[2048,1024]{0,1:T(8,128)(2,1)} async-done(((bf16[128,1024]{0,1:T(8,128)(2,1)}), bf16[2048,1024]{0,1:T(8,128)(2,1)}) %all-gather.5.cloned.1.call-update) | async-done | bytes 4194320 | tf_op jit(solution)/shard_map/all_gather | solution.py:91
  88.6 76.0 %all-gather.7.cloned.1.call-done = bf16[2048,1024]{0,1:T(8,128)(2,1)} async-done(((bf16[128,1024]{0,1:T(8,128)(2,1)}), bf16[2048,1024]{0,1:T(8,128)(2,1)}) %all-gather.7.cloned.1.call-update) | async-done | bytes 4194320 | tf_op jit(solution)/shard_map/all_gather | solution.py:92
  164.6 69.2 %while.38 = (s32[]{:T(128)}, f32[128,1024]{0,1:T(8,128)S(1)}, s32[4]{0:T(128)S(1)}, bf16[2048,1024]{0,1:T(8,128)(2,1)}, bf16[128,1024]{1,0:T(8,128)(2,1)}, /*ind...) while((s32[]{:T(128)}, f32[128,1024]{0,1:T(8,128)S(1)}, s32[4]{0:T(128)S(1)}, ...), condition=%wide.region_7.8_spmd.clone, body=%wide.region_1.7_spmd.clone.sunk | while | flops 68331264 | bytes 4070629 | solution.py:55
  166.2 2.7 conditional.8
  167.3 1.5 fusion.5
  170.5 2.7 conditional.8
  171.6 1.5 fusion.5
  174.8 2.7 conditional.8
  176.0 1.5 fusion.5
  179.2 2.7 conditional.8
  180.3 1.5 fusion.5
  183.5 2.7 conditional.8
  184.6 1.5 fusion.5
  187.8 2.7 conditional.8
  188.9 1.5 fusion.5
  192.2 2.7 conditional.8
  193.3 1.5 fusion.5
  196.5 2.7 conditional.8
  197.6 1.5 fusion.5
  200.8 2.7 conditional.8
  201.9 1.5 fusion.5
  205.1 2.7 conditional.8
  206.2 1.5 fusion.5
  209.4 2.7 conditional.8
  210.6 1.5 fusion.5
  213.8 2.7 conditional.8
  214.9 1.5 fusion.5
  218.1 2.7 conditional.8
  219.2 1.5 fusion.5
  222.4 2.7 conditional.8
  223.5 1.5 fusion.5
  226.7 2.7 conditional.8
  227.8 1.5 fusion.5
  231.0 2.7 conditional.8
  232.1 1.5 fusion.5
  235.9 92.4 %while.39 = (s32[]{:T(128)}, f32[128,1024]{0,1:T(8,128)S(1)}, s32[4]{0:T(128)S(1)}, bf16[2048,1024]{0,1:T(8,128)(2,1)}, bf16[128,1024]{1,0:T(8,128)(2,1)}, /*ind...) while((s32[]{:T(128)}, f32[128,1024]{0,1:T(8,128)S(1)}, ...), condition=%wide.region_18.19_spmd.clone, body=%wide.region_12.18_spmd.clone.sunk | while | flops 102541056 | bytes 6692085 | solution.py:55
  237.5 4.1 conditional.9
  243.3 4.1 conditional.9
  249.0 4.1 conditional.9
  254.8 4.1 conditional.9
  260.5 4.2 conditional.9
  266.3 4.1 conditional.9
  268.9 1.5 fusion.20
  272.1 4.1 conditional.9
  277.9 4.1 conditional.9
  283.6 4.1 conditional.9
  289.4 4.2 conditional.9
  295.3 4.2 conditional.9
  297.9 1.5 fusion.20
  301.1 4.2 conditional.9
  303.7 1.5 fusion.20
  306.8 4.1 conditional.9
  312.6 4.1 conditional.9
  318.4 4.1 conditional.9
  324.1 4.1 conditional.9
  329.1 102.2 %psum.7 = f32[1024]{0:T(1024)} all-reduce(f32[1024]{0:T(1024)S(1)} %get-tuple-element.696), channel_id=1, replica_groups=mesh['dp'=32,'ctx'=16] {'dp','ctx'}, use_global_device_ids=true, to_apply=%region_25.26 | all-reduce | flops 1024 | bytes 8192 | tf_op jit(solution)/shard_map/psum | solution.py:104
  431.3 33.2 %conditional.3 = (bf16[128,1024]{1,0:T(8,128)(2,1)S(1)}, bf16[128,1024]{1,0:T(8,128)(2,1)S(1)}) conditional(s32[]{:T(128)} %convert_element_type.132, () %tuple.110, (bf16[2048,1024]{1,0:T(8,128)(2,1)}, bf16[128,1024]{1,0:T(8,128)(2,1)}, bf16[2048,1024]{0,1:T(8,128)(2,1)}, bf16[128,1024]{1,0:T(8,128)(2,1)S(1)}, f32[2048,128]{1,0:T(8,128)S(1)}) %tuple.196), branch_computations={%region_22.23_spmd, %region_23.24_spmd} | conditional | flops 2187591680 | bytes 55574572 | solution.py:172
  431.5 6.5 %copy.84 = bf16[2048,1024]{0,1:T(8,128)(2,1)} copy(bf16[2048,1024]{1,0:T(8,128)(2,1)} %get-tuple-element.680) | data formatting | bytes 8388608 | tf_op jit(solution)/shard_map
  438.0 6.9 %fusion.34 = f32[8,2048,128]{2,1,0:T(8,128)} fusion(bf16[2048,8,128]{0,2,1:T(8,128)(2,1)} %bitcast.99, bf16[128,1024]{1,0:T(8,128)(2,1)S(1)} %get-tuple-element.578), kind=kOutput, calls=%fused_computation.42 | convolution fusion | flops 536870912 | bytes 12845056 | tf_op jit(solution)/shard_map/cond/branch_1_fun/rhd,chd->hrc/dot_general | solution.py:38
  444.9 11.4 %fusion.33 = bf16[8,128,128]{1,2,0:T(8,128)(2,1)S(1)} fusion(bf16[2048,8,128]{0,2,1:T(8,128)(2,1)} %bitcast.100, f32[8,2048,128]{2,1,0:T(8,128)} %fusion.34, bf16[2048,8,128]{0,2,1:T(8,128)(2,1)} %bitcast.101, f32[2048,128]{1,0:T(8,128)S(1)} %get-tuple-element.579, bf16[128,1024]{1,0:T(8,128)(2,1)S(1)} %copy-done.3), kind=kOutput, calls=%fused_computation.41 | convolution fusion | flops 1099038720 | bytes 18350080 | tf_op jit(solution)/shard_map/cond/branch_1_fun/hrc,rhd->chd/dot_general | solution.py:167
  456.3 8.0 %fusion.32 = bf16[8,128,128]{1,2,0:T(8,128)(2,1)S(1)} fusion(bf16[2048,8,128]{0,2,1:T(8,128)(2,1)} %bitcast.102, f32[8,2048,128]{2,1,0:T(8,128)} %fusion.34, f32[2048,128]{1,0:T(8,128)S(1)} %get-tuple-element.579), kind=kOutput, calls=%fused_computation.40 | convolution fusion | flops 551682048 | bytes 13893632 | tf_op jit(solution)/shard_map/cond/branch_1_fun/hrc,rhd->chd/dot_general | solution.py:164
  (281 shorter events, 116.9 us)
Async XLA Ops:
  7.2 81.4 %all-gather.5.cloned.1.call-start = ((), (), s32[]{:S(2)}) async-start(), calls=%async_computation | async-start | bytes 4456448 | tf_op jit(solution)/shard_map/all_gather | solution.py:91
  9.0 155.5 %all-gather.7.cloned.1.call-start = ((), (), s32[]{:S(2)}) async-start(), calls=%async_computation.1 | async-start | bytes 4456448 | tf_op jit(solution)/shard_map/all_gather | solution.py:92
  10.9 420.4 %all-gather.11.cloned.1.call-start = ((), (), s32[]{:S(2)}) async-start(), calls=%async_computation.3 | async-start | bytes 4456448 | tf_op jit(solution)/shard_map/all_gather | solution.py:145
  12.8 418.5 %all-gather.9.cloned.1.call-start = ((), (), s32[]{:S(2)}) async-start(), calls=%async_computation.2 | async-start | bytes 4456448 | tf_op jit(solution)/shard_map/all_gather | solution.py:146
  164.6 69.8 %copy-start.1 = (bf16[128,1024]{1,0:T(8,128)(2,1)S(1)}, bf16[128,1024]{1,0:T(8,128)(2,1)}, u32[]{:S(2)}) copy-start(bf16[128,1024]{1,0:T(8,128)(2,1)} %param.20) | copy-start | bytes 786436
  164.6 69.8 %copy-start.2 = (bf16[128,1024]{1,0:T(8,128)(2,1)S(1)}, bf16[128,1024]{1,0:T(8,128)(2,1)}, u32[]{:S(2)}) copy-start(bf16[128,1024]{1,0:T(8,128)(2,1)} %param.21) | copy-start | bytes 786436
  164.6 69.8 %copy-start.6 = (f32[1024]{0:T(1024)S(1)}, f32[1024]{0:T(1024)}, u32[]{:S(2)}) copy-start(f32[1024]{0:T(1024)} %param.22) | copy-start | bytes 12292
  235.9 195.4 %copy-start = (bf16[128,1024]{1,0:T(8,128)(2,1)S(1)}, bf16[128,1024]{1,0:T(8,128)(2,1)}, u32[]{:S(2)}) copy-start(bf16[128,1024]{1,0:T(8,128)(2,1)} %param.18) | copy-start | bytes 786436
  438.0 6.9 %copy-start.3 = (bf16[128,1024]{1,0:T(8,128)(2,1)S(1)}, bf16[128,1024]{1,0:T(8,128)(2,1)}, u32[]{:S(2)}) copy-start(bf16[128,1024]{1,0:T(8,128)(2,1)} %get-tuple-element.576) | copy-start | bytes 786436 | tf_op jit(solution)/shard_map/cond
  464.5 0.7 copy-start.4
  464.6 0.8 copy-start.5
Sparse Core Ops, SparseCore 0:
  11.6 76.9 all-gather.4
  92.1 72.3 all-gather.6
  167.5 72.6 all-gather.10
  243.6 66.3 all-gather.8
where the time goes:
time: 476 us; the launch traced here: 472 us
  waiting for transfers between devices  148 us (31%)
  blocking collectives  102 us (21%)
  matrix products  94 us (20%)
  local copies, waits for them, and re-layouts  51.9 us (11%)
  other arithmetic  37.2 us (8%)
  loops' own time  23.7 us (5%)
  between operations  14.6 us (3%)
    psum x1, blocking collectives, body(): grad_gain = lax.psum(jnp.sum(normed * grads * gates, axis=0), ('dp', 'ctx'))  102 us
    all_gather x1, waiting for transfers between devices, body(): lax.all_gather(value_vectors, 'ctx', axis=0, tiled=True)  76 us
    all_gather x1, waiting for transfers between devices, body(): lax.all_gather(key_vectors, 'ctx', axis=0, tiled=True)  72.1 us
    dynamic_slice x32, local copies, waits for them, and re-layouts, fold_step(): lax.dynamic_slice_in_dim(array, offset, row_count, 0)  34.7 us
    dot_general x17, matrix products, head_scores(): jnp.einsum('rhd,chd->hrc', head_split(left), head_split(right), preferred...  27.4 us
    dot_general x16, matrix products, forward_work(): jnp.einsum('hrc,chd->rhd', weights, head_split(value_part), preferred_ele...  24 us
    dot_general x16, matrix products, query_work(): jnp.einsum('hrc,chd->rhd', grad_scores, head_split(key_part), preferred_e...  23.2 us
    another operation x2, loops' own time, fold_shards(): return lax.fori_loop(0, shard_count, fold_step, initial)  22.1 us
  transfers between devices with their start and end apart: 4, of which 2 were waited for; matrix products, arithmetic and copies ran while one was open for 31% of the time, Pallas kernels for 0%

commit v1 on v0

v1 whole, which is shorter than its diff:
```python
import functools
import math

import jax
import jax.numpy as jnp
from jax import lax
from jax.experimental import pallas as pl
from jax.experimental.pallas import tpu as pltpu
from jax.sharding import PartitionSpec as P

HEAD = 128
EPSILON = 1e-05
PEERS = 16
CHUNK = 64
HALF = PEERS * CHUNK
BLOCK = 256
WINDOW = HALF + BLOCK
STEPS = HALF // BLOCK
SCALE = 1.0 / math.sqrt(HEAD)

QUERY, KEY_E, KEY_L, VAL_E, VAL_L, ATT, GRAD, DQ, DK_E, DK_L, DV_E, DV_L = range(12)
KINDS = 12


def contract(left, right, left_axis, right_axis):
    return lax.dot_general(
        left, right, (((left_axis,), (right_axis,)), ((), ())), preferred_element_type=jnp.float32
    )


def attention_kernel(
    lengths,
    queries,
    keys,
    values,
    gates,
    cotangent,
    gain,
    output,
    grad_queries,
    grad_keys,
    grad_values,
    gain_part,
    q_all,
    k_all,
    v_all,
    weights,
    slopes,
    att_out,
    att_in,
    grad_out,
    grad_in,
    dq_out,
    dq_in,
    dk_sum,
    dv_sum,
    dk_out,
    dv_out,
    dk_early,
    dk_late,
    dv_early,
    dv_late,
    send_sem,
    recv_sem,
):
    me = lax.axis_index("ctx")
    head = me // 2
    role = me % 2

    def columns(which):
        return pl.ds(pl.multiple_of(which * HEAD, HEAD), HEAD)

    def rows_at(start, size=CHUNK):
        return pl.ds(pl.multiple_of(start, CHUNK), size)

    def remote(src, dst, kind, target, source):
        return pltpu.make_async_remote_copy(
            src_ref=src,
            dst_ref=dst,
            send_sem=send_sem.at[kind, target],
            recv_sem=recv_sem.at[kind, source],
            device_id={"ctx": target},
            device_id_type=pl.DeviceIdType.MESH,
        )

    def push(src, dst, kind, target):
        @pl.when(target != me)
        def _():
            remote(src, dst, kind, target, me).start()

        @pl.when(target == me)
        def _():
            dst[...] = src[...]

    def arrived(buffer, kind, source):
        @pl.when(source != me)
        def _():
            remote(buffer, buffer, kind, source, source).wait_recv()

    def sent(buffer, kind, target):
        @pl.when(target != me)
        def _():
            remote(buffer, buffer, kind, target, me).wait_send()

    def each_peer(work):
        def step(turn, carry):
            work(lax.rem(me + turn, PEERS))
            return carry

        lax.fori_loop(0, PEERS, step, 0)

    barrier = pltpu.get_barrier_semaphore()

    def greet(turn, carry):
        pl.semaphore_signal(
            barrier,
            inc=1,
            device_id={"ctx": lax.rem(me + turn, PEERS)},
            device_id_type=pl.DeviceIdType.MESH,
        )
        return carry

    lax.fori_loop(1, PEERS, greet, 0)

    @pl.when(role == 0)
    def _():
        k_all[:HALF, :] = jnp.zeros((HALF, HEAD), jnp.bfloat16)
        v_all[:HALF, :] = jnp.zeros((HALF, HEAD), jnp.bfloat16)

    pl.semaphore_wait(barrier, PEERS - 1)

    def chunk_of(shard, kind_role):
        return jnp.where(kind_role == 0, shard, PEERS - 1 - shard)

    piece = q_all.at[:CHUNK, :]

    def send_queries_keys(peer):
        peer_role, cols = peer % 2, columns(peer // 2)
        push(
            queries.at[rows_at(peer_role * CHUNK), cols],
            q_all.at[rows_at(chunk_of(me, peer_role) * CHUNK), :],
            QUERY,
            peer,
        )
        push(
            keys.at[:CHUNK, cols],
            k_all.at[rows_at(me * CHUNK + (1 - peer_role) * HALF), :],
            KEY_E,
            peer,
        )

        @pl.when(peer_role == 1)
        def _():
            push(
                keys.at[CHUNK:, cols],
                k_all.at[rows_at((2 * PEERS - 1 - me) * CHUNK), :],
                KEY_L,
                peer,
            )

    def send_values(peer):
        peer_role, cols = peer % 2, columns(peer // 2)
        push(
            values.at[:CHUNK, cols],
            v_all.at[rows_at(me * CHUNK + (1 - peer_role) * HALF), :],
            VAL_E,
            peer,
        )

        @pl.when(peer_role == 1)
        def _():
            push(
                values.at[CHUNK:, cols],
                v_all.at[rows_at((2 * PEERS - 1 - me) * CHUNK), :],
                VAL_L,
                peer,
            )

    each_peer(send_queries_keys)
    each_peer(send_values)

    def wait_queries_keys(peer):
        arrived(piece, QUERY, peer)
        arrived(piece, KEY_E, peer)

        @pl.when(role == 1)
        def _():
            arrived(piece, KEY_L, peer)

    def wait_values(peer):
        arrived(piece, VAL_E, peer)

        @pl.when(role == 1)
        def _():
            arrived(piece, VAL_L, peer)

    each_peer(wait_queries_keys)

    ends = []
    total = 0
    for user in range(lengths.shape[1]):
        total = total + lengths[0, user]
        ends.append(total)

    def score_step(step, carry):
        rows = pl.ds(pl.multiple_of(step * BLOCK, BLOCK), BLOCK)
        q_block = q_all[rows, :]
        q_time = role * HALF + step * BLOCK + lax.broadcasted_iota(jnp.int32, (BLOCK, 1), 0)
        first = jnp.zeros((BLOCK, 1), jnp.int32)
        for end in ends:
            first = jnp.where(q_time >= end, end, first)
        for part in range(WINDOW // BLOCK):
            start = step * BLOCK + part * BLOCK
            k_block = k_all[pl.ds(pl.multiple_of(start, BLOCK), BLOCK), :]
            k_time = (
                start - (1 - role) * HALF + lax.broadcasted_iota(jnp.int32, (1, BLOCK), 1)
            )
            scores = contract(q_block, k_block, 1, 1) * SCALE
            live = (k_time >= first) & (k_time <= q_time)
            sigmoid = 0.5 * jnp.tanh(0.5 * scores) + 0.5
            silu = scores * sigmoid
            slope = (sigmoid + silu * (1.0 - sigmoid)) * SCALE
            cols = slice(part * BLOCK, (part + 1) * BLOCK)
            weights[rows, cols] = jnp.where(live, silu, 0.0).astype(jnp.bfloat16)
            slopes[rows, cols] = jnp.where(live, slope, 0.0)
        return carry

    lax.fori_loop(0, STEPS, score_step, 0)

    each_peer(wait_values)

    def attend_step(step, carry):
        rows = pl.ds(pl.multiple_of(step * BLOCK, BLOCK), BLOCK)
        window = pl.ds(pl.multiple_of(step * BLOCK, BLOCK), WINDOW)
        att_out[rows, :] = contract(weights[rows, :], v_all[window, :], 1, 0).astype(jnp.bfloat16)
        for part in range(BLOCK // CHUNK):
            chunk = step * (BLOCK // CHUNK) + part
            push(
                att_out.at[rows_at(chunk * CHUNK), :],
                att_in.at[rows_at(role * CHUNK), columns(head)],
                ATT,
                chunk_of(chunk, role),
            )
        return carry

    lax.fori_loop(0, STEPS, attend_step, 0)

    gain_row = gain[...]
    gain_sum = jnp.zeros((1, gain.shape[1]), jnp.float32)
    each_peer(lambda peer: arrived(piece, ATT, peer))
    for part in range(4):
        rows = slice(part * 32, part * 32 + 32)
        attended = att_in[rows, :].astype(jnp.float32)
        centered = attended - jnp.mean(attended, axis=1, keepdims=True)
        variance = jnp.mean(centered * centered, axis=1, keepdims=True)
        inverse = lax.rsqrt(variance + EPSILON)
        normed = centered * inverse
        gate = gates[rows, :].astype(jnp.float32)
        grad = cotangent[rows, :].astype(jnp.float32)
        scaled = gate * gain_row
        output[rows, :] = (normed * scaled).astype(jnp.bfloat16)
        gain_sum = gain_sum + jnp.sum(normed * grad * gate, axis=0, keepdims=True)
        grad = grad * scaled
        grad_out[rows, :] = (
            (
                grad
                - jnp.mean(grad, axis=1, keepdims=True)
                - normed * jnp.mean(grad * normed, axis=1, keepdims=True)
            )
            * inverse
        ).astype(jnp.bfloat16)
    gain_part[...] = gain_sum

    def send_grad(peer):
        peer_role = peer % 2
        push(
            grad_out.at[rows_at(peer_role * CHUNK), columns(peer // 2)],
            grad_in.at[rows_at(chunk_of(me, peer_role) * CHUNK), :],
            GRAD,
            peer,
        )

    each_peer(send_grad)
    dk_sum[...] = jnp.zeros(dk_sum.shape, jnp.float32)
    dv_sum[...] = jnp.zeros(dv_sum.shape, jnp.float32)

    def backward_step(turn, carry):
        step = STEPS - 1 - turn
        for part in range(BLOCK // CHUNK):
            arrived(piece, GRAD, chunk_of(step * (BLOCK // CHUNK) + part, role))
        rows = pl.ds(pl.multiple_of(step * BLOCK, BLOCK), BLOCK)
        grad = grad_in[rows, :]
        q_block = q_all[rows, :]
        dq = jnp.zeros((BLOCK, HEAD), jnp.float32)
        for part in range(WINDOW // BLOCK):
            window = pl.ds(pl.multiple_of(step * BLOCK + part * BLOCK, BLOCK), BLOCK)
            cols = slice(part * BLOCK, (part + 1) * BLOCK)
            grad_weights = contract(grad, v_all[window, :], 1, 1)
            grad_scores = (grad_weights * slopes[rows, cols]).astype(jnp.bfloat16)
            dq = dq + contract(grad_scores, k_all[window, :], 1, 0)
            dk_sum[window, :] += contract(grad_scores, q_block, 0, 0)
            dv_sum[window, :] += contract(weights[rows, cols], grad, 0, 0)
        dq_out[rows, :] = dq.astype(jnp.bfloat16)
        for part in range(BLOCK // CHUNK):
            chunk = step * (BLOCK // CHUNK) + part
            push(
                dq_out.at[rows_at(chunk * CHUNK), :],
                dq_in.at[rows_at(role * CHUNK), columns(head)],
                DQ,
                chunk_of(chunk, role),
            )
        return carry

    lax.fori_loop(0, STEPS, backward_step, 0)
    dk_out[...] = dk_sum[...].astype(jnp.bfloat16)
    dv_out[...] = dv_sum[...].astype(jnp.bfloat16)

    def send_key_grads(peer):
        early = rows_at(peer * CHUNK + (1 - role) * HALF)
        slot = rows_at(role * CHUNK)
        push(dk_out.at[early, :], dk_early.at[slot, columns(head)], DK_E, peer)
        push(dv_out.at[early, :], dv_early.at[slot, columns(head)], DV_E, peer)

        @pl.when(role == 1)
        def _():
            late = rows_at((2 * PEERS - 1 - peer) * CHUNK)
            push(dk_out.at[late, :], dk_late.at[:, columns(head)], DK_L, peer)
            push(dv_out.at[late, :], dv_late.at[:, columns(head)], DV_L, peer)

    each_peer(send_key_grads)

    each_peer(lambda peer: arrived(piece, DQ, peer))
    grad_queries[...] = dq_in[...]

    def wait_key_grads(peer):
        arrived(piece, DK_E, peer)
        arrived(piece, DV_E, peer)

        @pl.when(peer % 2 == 1)
        def _():
            arrived(piece, DK_L, peer)
            arrived(piece, DV_L, peer)

    each_peer(wait_key_grads)

    def summed(early):
        return (early[:CHUNK, :].astype(jnp.float32) + early[CHUNK:, :].astype(jnp.float32)).astype(
            jnp.bfloat16
        )

    grad_keys[:CHUNK, :] = summed(dk_early)
    grad_keys[CHUNK:, :] = dk_late[...]
    grad_values[:CHUNK, :] = summed(dv_early)
    grad_values[CHUNK:, :] = dv_late[...]

    def drain(peer):
        for kind in (QUERY, KEY_E, VAL_E, ATT, GRAD, DQ, DK_E, DV_E):
            sent(piece, kind, peer)

        @pl.when(peer % 2 == 1)
        def _():
            sent(piece, KEY_L, peer)
            sent(piece, VAL_L, peer)

        @pl.when(role == 1)
        def _():
            sent(piece, DK_L, peer)
            sent(piece, DV_L, peer)

    each_peer(drain)


def body(queries, key_vectors, value_vectors, gate_values, cotangent, norm_gain, lengths):
    row_count, width = queries.shape
    wide = jax.ShapeDtypeStruct((row_count, width), jnp.bfloat16)
    vmem = pl.BlockSpec(memory_space=pltpu.VMEM)
    half16 = pltpu.VMEM((HALF, HEAD), jnp.bfloat16)
    full16 = pltpu.VMEM((2 * HALF, HEAD), jnp.bfloat16)
    full32 = pltpu.VMEM((2 * HALF, HEAD), jnp.float32)
    rows16 = pltpu.VMEM((row_count, width), jnp.bfloat16)
    chunk16 = pltpu.VMEM((CHUNK, width), jnp.bfloat16)
    output, grad_queries, grad_keys, grad_values, gain_part = pl.pallas_call(
        attention_kernel,
        out_shape=(wide, wide, wide, wide, jax.ShapeDtypeStruct((1, width), jnp.float32)),
        in_specs=[pl.BlockSpec(memory_space=pltpu.SMEM)] + [vmem] * 6,
        out_specs=(vmem,) * 5,
        scratch_shapes=[
            half16,
            full16,
            full16,
            pltpu.VMEM((HALF, WINDOW), jnp.bfloat16),
            pltpu.VMEM((HALF, WINDOW), jnp.float32),
            half16,
            rows16,
            rows16,
            half16,
            half16,
            rows16,
            full32,
            full32,
            full16,
            full16,
            rows16,
            chunk16,
            rows16,
            chunk16,
            pltpu.SemaphoreType.DMA((KINDS, PEERS)),
            pltpu.SemaphoreType.DMA((KINDS, PEERS)),
        ],
        compiler_params=pltpu.CompilerParams(
            collective_id=0, has_side_effects=True, vmem_limit_bytes=48 * 2**20
        ),
    )(lengths, queries, key_vectors, value_vectors, gate_values, cotangent, norm_gain.reshape(1, width))
    grad_gain = lax.psum(gain_part[0], ("dp", "ctx"))
    return output, grad_queries, grad_keys, grad_values, grad_gain


def solution(mesh):
    rows = P(("dp", "ctx"), None)
    return jax.shard_map(
        body,
        mesh=mesh,
        in_specs=(rows,) * 5 + (P(), P("dp", None)),
        out_specs=(rows,) * 4 + (P(),),
        check_vma=False,
    )
```

time: 476 us -> 180 us (0.38)
  waiting for transfers between devices: 148 us -> 0 us
  matrix products: 94 us -> 0 us
  Pallas kernels: 0 us -> 58.5 us
  local copies, waits for them, and re-layouts: 51.9 us -> 8.89 us
  other arithmetic: 37.2 us -> 0 us
  loops' own time: 23.7 us -> 0 us
  between operations: 14.6 us -> 0.66 us
  blocking collectives: 102 us -> 109 us
    all_gather x4 -> x0, waiting for transfers between devices: 148 us -> none  [the longest x1 76 us: body(): lax.all_gather(value_vectors, 'ctx', axis=0, tiled=True)]
    dot_general x51 -> x0, matrix products: 94 us -> none  [the longest x17 27.4 us: head_scores(): jnp.einsum('rhd,chd->hrc', head_split(left), head_split(right), preferred...]
    pallas_call x0 -> x1, Pallas kernels: none -> 58.5 us  [body(): pl.pallas_call(attention_kernel, out_shape=(wide, wide, wide, wide, jax.S...]
    dynamic_slice x32 -> x0, local copies, waits for them, and re-layouts: 34.7 us -> none  [fold_step(): lax.dynamic_slice_in_dim(array, offset, row_count, 0)]
    reduce_or x33 -> x0, other arithmetic: 24.9 us -> none  [the longest x16 11.8 us: query_fold(): return lax.cond(jnp.any(live > 0.0), query_work, keep_carry, running)]
    another operation x35 -> x0, loops' own time: 23.7 us -> none  [the longest x2 22.1 us: fold_shards(): return lax.fori_loop(0, shard_count, fold_step, initial)]
    psum x1, blocking collectives: 102 us -> 109 us  [body(): grad_gain = lax.psum(gain_part[0], ('dp', 'ctx'))]
    another operation x1 -> x0, local copies, waits for them, and re-layouts: 6.5 us -> none
  transfers between devices with their start and end apart: 4 -> 0, of which waited for: 2 -> 0; matrix products, arithmetic and copies ran while one was open for 31% -> 0% of each run, Pallas kernels for 0% -> 0%
where the time goes in v1:
time: 180 us; the launch traced here: 177 us
  blocking collectives  109 us (61%)
  Pallas kernels  58.5 us (32%)
  local copies, waits for them, and re-layouts  8.89 us (5%)
    psum x1, blocking collectives, body(): grad_gain = lax.psum(gain_part[0], ('dp', 'ctx'))  109 us
    pallas_call x1, Pallas kernels, body(): pl.pallas_call(attention_kernel, out_shape=(wide, wide, wide, wide, jax.S...  58.5 us
    unnamed x18, local copies, waits for them, and re-layouts  8.89 us

profile of v1, /device:TPU:6, one launch (start us, length us, event | category | flops | bytes accessed | tf_op | source)
XLA Modules:
  0.0 176.9 jit_solution(1033868325927905438)
XLA Ops:
  0.6 0.0 copy-start.6
  0.6 0.6 copy-done.6
  1.3 0.0 copy-start
  1.3 0.9 copy-done
  2.2 0.0 copy-start.1
  2.2 0.9 copy-done.1
  3.2 0.0 copy-start.2
  3.2 0.9 copy-done.2
  4.1 0.0 copy-start.3
  4.1 0.9 copy-done.3
  5.1 0.0 copy-start.4
  5.1 0.9 copy-done.4
  6.0 0.0 copy-start.5
  6.0 0.7 copy-done.5
  6.7 58.5 %shard_map.110 = (bf16[128,1024]{1,0:T(8,128)(2,1)S(1)}, bf16[128,1024]{1,0:T(8,128)(2,1)S(1)}, bf16[128,1024]{1,0:T(8,128)(2,1)S(1)}, bf16[128,1024]{1,0:T(8,128)(2,1)S(1)}, f32[1,1024]{1,0:T(1,128)S(1)}) custom-call(s32[1,4]{1,0:T(1,128)S(1)} %copy-done.6, bf16[128,1024]{1,0:T(8,128)(2,1)S(1)} %copy-done, bf16[128,1024]{1,0:T(8,128)(2,1)S(1)} %copy-done.1, ...), custom_call_target="tpu_custom_call" | custom-call | tf_op jit(solution)/shard_map/pallas_call | solution.py:382
  65.3 108.8 %psum.7 = f32[1024]{0:T(1024)} all-reduce(f32[1024]{0:T(1024)S(1)} %bitcast.3), channel_id=1, replica_groups=mesh['dp'=32,'ctx'=16] {'dp','ctx'}, use_global_device_ids=true, to_apply=%region_0.0 | all-reduce | flops 1024 | bytes 8192 | tf_op jit(solution)/shard_map/psum | solution.py:414
  174.1 0.7 copy.16
  174.8 0.7 copy.17
  175.5 0.7 copy.18
  176.2 0.7 copy.19
Async XLA Ops:
  0.6 0.7 copy-start.6
  1.3 0.9 copy-start
  2.2 0.9 copy-start.1
  3.2 0.9 copy-start.2
  4.1 0.9 copy-start.3
  5.1 0.9 copy-start.4
  6.0 0.7 copy-start.5

commit v2 on v0

v2 whole, which is shorter than its diff:
```python
import math

import jax
import jax.numpy as jnp
from jax import lax
from jax.experimental import pallas as pl
from jax.experimental.pallas import tpu as pltpu
from jax.sharding import PartitionSpec as P

HEAD = 128
EPSILON = 1e-05
PEERS = 16
HEADS = 8
CHUNK = 64
HALF = PEERS * CHUNK
BLOCK = 256
PER_BLOCK = BLOCK // CHUNK
STEPS = HALF // BLOCK
PARTS = STEPS + 1
SCALE = 1.0 / math.sqrt(HEAD)
STAGGER = True

QUERY, KEY, VALUE, ATT, GRAD, BACK, BACK_E, GAIN = range(8)
KINDS = 8
MESH = pl.DeviceIdType.MESH


def contract(left, right, left_axis, right_axis):
    return lax.dot_general(
        left, right, (((left_axis,), (right_axis,)), ((), ())), preferred_element_type=jnp.float32
    )


def gain_stages(groups):
    stages, stride, slot = [], 1, PEERS
    while stride < groups:
        size = min(4, groups // stride)
        stages.append((slot, stride, size))
        slot, stride = slot + size, stride * size
    return stages, slot


def attention_kernel(
    groups,
    lengths_hbm,
    queries_hbm,
    keys_hbm,
    values_hbm,
    gates_hbm,
    cotangent_hbm,
    gain_hbm,
    output,
    grad_queries,
    grad_keys,
    grad_values,
    gain_total,
    lengths,
    own,
    gates,
    cotangent,
    gain,
    box,
    weights,
    slopes,
    att_out,
    att_in,
    grad_out,
    grad_in,
    sums,
    out_box,
    back_early,
    back_late,
    gain_slots,
    local_sem,
    send_sem,
    recv_sem,
    gain_send_sem,
    gain_recv_sem,
    go_sem,
):
    me = lax.axis_index("ctx")
    group = lax.axis_index("dp")
    core = group % 2
    head = me // 2
    role = (me + core) % 2
    stages, _ = gain_stages(groups)

    staged = [
        pltpu.make_async_copy(src, dst, local_sem.at[index])
        for index, (src, dst) in enumerate(
            (
                (queries_hbm, own.at[0]),
                (keys_hbm, own.at[1]),
                (values_hbm, own.at[2]),
                (lengths_hbm, lengths),
                (gates_hbm, gates),
                (cotangent_hbm, cotangent),
                (gain_hbm, gain),
            )
        )
    ]
    for copy in staged:
        copy.start()

    def columns(which):
        return pl.ds(pl.multiple_of(which * HEAD, HEAD), HEAD)

    def remote(src, dst, kind, kind_role, target):
        return pltpu.make_async_remote_copy(
            src_ref=src,
            dst_ref=dst,
            send_sem=send_sem.at[kind, kind_role],
            recv_sem=recv_sem.at[kind, kind_role],
            device_id={"ctx": target},
            device_id_type=MESH,
        )

    def push(src, dst, kind, kind_role, target):
        remote(src, dst, kind, kind_role, target).start()

    def landed(ref, kind, kind_role):
        remote(ref, ref, kind, kind_role, me).wait_recv()

    def left(ref, kind, kind_role):
        remote(ref, ref, kind, kind_role, me).wait_send()

    def worker(which, kind_role):
        return 2 * which + (kind_role + core) % 2

    def stage_peer(stride, size, turn):
        place = group // stride % size
        return group + ((place + turn) % size - place) * stride

    barrier = pltpu.get_barrier_semaphore()
    for turn in range(1, PEERS):
        pl.semaphore_signal(
            barrier, inc=1, device_id={"ctx": lax.rem(me + turn, PEERS)}, device_id_type=MESH
        )
    greeted = PEERS - 1
    for _, stride, size in stages:
        for turn in range(1, size):
            pl.semaphore_signal(
                barrier,
                inc=1,
                device_id={"dp": stage_peer(stride, size, turn)},
                device_id_type=MESH,
            )
            greeted += 1
    sums[...] = jnp.zeros(sums.shape, jnp.float32)
    for copy in staged[:4]:
        copy.wait()
    pl.semaphore_wait(barrier, greeted)

    @pl.when(role == 0)
    def _():
        box[:, 0, me] = own[:, 0, :, columns(head)]

    @pl.when(role == 1)
    def _():
        box[0, 1, me] = own[0, 1, :, columns(head)]
        box[1:, :, me] = own[1:, :, :, columns(head)]

    partner = group + 1 - 2 * core
    if STAGGER:

        @pl.when(core == 1)
        def _():
            pl.semaphore_wait(go_sem, 1)

    def each_worker(work):
        def step(turn, carry):
            which = lax.rem(head + turn, HEADS)

            @pl.when((turn > 0) | (role == 1))
            def _():
                work(which, 0, worker(which, 0))

            @pl.when((turn > 0) | (role == 0))
            def _():
                work(which, 1, worker(which, 1))

            return carry

        lax.fori_loop(0, HEADS, step, 0)

    def send_queries_keys(which, half, peer):
        cols = columns(which)
        push(own.at[0, half, :, cols], box.at[0, half, me], QUERY, half, peer)
        if half == 0:
            push(own.at[1, 0, :, cols], box.at[1, 0, me], KEY, 0, peer)
        else:
            push(own.at[1, :, :, cols], box.at[1, :, me], KEY, 1, peer)

    def send_values(which, half, peer):
        cols = columns(which)
        if half == 0:
            push(own.at[2, 0, :, cols], box.at[2, 0, me], VALUE, 0, peer)
        else:
            push(own.at[2, :, :, cols], box.at[2, :, me], VALUE, 1, peer)

    each_worker(send_queries_keys)
    each_worker(send_values)

    def by_role(work):
        for half in range(2):

            @pl.when(role == half)
            def _():
                work(half, HEADS - 1)

            @pl.when(role != half)
            def _():
                work(half, HEADS)

    def inputs_left():
        def wait(half, count):
            left(box.at[0, 0, :count], QUERY, half)
            if half == 0:
                left(box.at[1, 0, :count], KEY, 0)
                left(box.at[2, 0, :count], VALUE, 0)
            else:
                left(box.at[1, :, :count], KEY, 1)
                left(box.at[2, :, :count], VALUE, 1)

        by_role(wait)

    if STAGGER:

        @pl.when(core == 0)
        def _():
            inputs_left()
            pl.semaphore_signal(go_sem, inc=1, device_id={"dp": partner}, device_id_type=MESH)

    ends = []
    total = 0
    for user in range(lengths.shape[1]):
        total = total + lengths[0, user]
        ends.append(total)

    others = slice(0, PEERS - 1)

    @pl.when(role == 0)
    def _():
        landed(box.at[0, 0, others], QUERY, 0)
        landed(box.at[1, 0, others], KEY, 0)

    @pl.when(role == 1)
    def _():
        landed(box.at[0, 1, others], QUERY, 1)
        landed(box.at[1, :, others], KEY, 1)

    def rows_of(which, half, block):
        start = pl.multiple_of(block * PER_BLOCK, PER_BLOCK)
        return box[which, half, pl.ds(start, PER_BLOCK)].reshape(BLOCK, HEAD)

    def times(half, block, shape, axis):
        place = lax.broadcasted_iota(jnp.int32, shape, axis)
        chunk, inner = place // CHUNK, place % CHUNK
        shard = block * PER_BLOCK + chunk
        return jnp.where(half == 0, shard, 2 * PEERS - 1 - shard) * CHUNK + inner

    def key_block(step, part):
        early = (role == 0) | (part <= step)
        late_role = jnp.where(part <= step, 3 - step + part, part - 1)
        block = jnp.where(role == 0, min(part, STEPS - 1), late_role)
        return jnp.where(early, 0, 1), block

    def score_step(step, carry):
        q_block = rows_of(0, role, step)
        q_time = times(role, step, (BLOCK, 1), 0)
        first = jnp.zeros((BLOCK, 1), jnp.int32)
        for end in ends:
            first = jnp.where(q_time >= end, end, first)

        for part in range(PARTS):
            half, block = key_block(step, part)
            k_time = times(half, block, (1, BLOCK), 1)
            if part == STEPS:
                k_time = jnp.where(role == 0, 2 * HALF, k_time)
            raw = contract(q_block, rows_of(1, half, block), 1, 1)
            scores = raw * SCALE
            live = (k_time >= first) & (k_time <= q_time)
            sigmoid = 0.5 * jnp.tanh(raw * (0.5 * SCALE)) + 0.5
            silu = scores * sigmoid
            slope = sigmoid * SCALE + silu * (SCALE - SCALE * sigmoid)
            weights[step, part] = jnp.where(live, silu, 0.0).astype(jnp.bfloat16)
            slopes[step, part] = jnp.where(live, slope, 0.0)
        return carry

    lax.fori_loop(0, STEPS, score_step, 0)

    @pl.when(role == 0)
    def _():
        landed(box.at[2, 0, others], VALUE, 0)

    @pl.when(role == 1)
    def _():
        landed(box.at[2, :, others], VALUE, 1)

    def each_owner(step, work):
        for part in range(PER_BLOCK):
            shard = step * PER_BLOCK + part

            @pl.when(shard != me)
            def _():
                work(shard, False)

            @pl.when(shard == me)
            def _():
                work(shard, True)

    def deliver(src, dst, kind, target, here):
        if here:
            dst[...] = src[...]
        else:
            for half in range(2):

                @pl.when(role == half)
                def _():
                    push(src, dst, kind, half, target)

    def attend_step(step, carry):
        attended = jnp.zeros((BLOCK, HEAD), jnp.float32)
        for part in range(PARTS):
            half, block = key_block(step, part)
            attended = attended + contract(weights[step, part], rows_of(2, half, block), 1, 0)
        start = pl.multiple_of(step * PER_BLOCK, PER_BLOCK)
        att_out[pl.ds(start, PER_BLOCK)] = attended.astype(jnp.bfloat16).reshape(
            PER_BLOCK, CHUNK, HEAD
        )
        each_owner(
            step,
            lambda shard, here: deliver(
                att_out.at[shard], att_in.at[role, :, columns(head)], ATT, shard, here
            ),
        )
        return carry

    lax.fori_loop(0, STEPS, attend_step, 0)
    for copy in staged[4:]:
        copy.wait()
    gain_row = gain[...]
    by_role(lambda half, count: landed(att_in.at[half, :, : count * HEAD], ATT, half))

    def normalize(part, gain_sum):
        half, rows = part // 2, pl.ds(pl.multiple_of(part % 2 * 32, 32), 32)
        attended = att_in[half, rows, :].astype(jnp.float32)
        centered = attended - jnp.mean(attended, axis=1, keepdims=True)
        variance = jnp.mean(centered * centered, axis=1, keepdims=True)
        inverse = lax.rsqrt(variance + EPSILON)
        normed = centered * inverse
        gate = gates[half, rows, :].astype(jnp.float32)
        grad = cotangent[half, rows, :].astype(jnp.float32)
        scaled = gate * gain_row
        output[half, rows, :] = (normed * scaled).astype(jnp.bfloat16)
        gain_sum = gain_sum + jnp.sum(normed * grad * gate, axis=0, keepdims=True)
        grad = grad * scaled
        grad_out[half, rows, :] = (
            (
                grad
                - jnp.mean(grad, axis=1, keepdims=True)
                - normed * jnp.mean(grad * normed, axis=1, keepdims=True)
            )
            * inverse
        ).astype(jnp.bfloat16)
        return gain_sum

    gain_sum = lax.fori_loop(0, 4, normalize, jnp.zeros(gain_row.shape, jnp.float32))

    grad_in[me] = grad_out[role, :, columns(head)]
    each_worker(
        lambda which, half, peer: push(
            grad_out.at[half, :, columns(which)], grad_in.at[me], GRAD, half, peer
        )
    )

    def gain_copy(slot, stage, target):
        return pltpu.make_async_remote_copy(
            src_ref=slot,
            dst_ref=slot,
            send_sem=gain_send_sem.at[stage],
            recv_sem=gain_recv_sem.at[stage],
            device_id={"dp": target},
            device_id_type=MESH,
        )

    for which in range(HEADS):
        gain_slots[me, which : which + 1, :] = gain_sum[:, which * HEAD : (which + 1) * HEAD]

    def send_gain(turn, carry):
        push(gain_slots.at[me], gain_slots.at[me], GAIN, 0, lax.rem(me + turn, PEERS))
        return carry

    lax.fori_loop(1, PEERS, send_gain, 0)

    def gain_send(stage, total):
        slot, stride, size = stages[stage]
        mine = slot + group // stride % size
        gain_slots[mine] = total
        for turn in range(1, size):
            gain_copy(gain_slots.at[mine], stage, stage_peer(stride, size, turn)).start()

    def gain_stage_sum(stage):
        slot, stride, size = stages[stage]
        gain_copy(gain_slots.at[slot : slot + size - 1], stage, group).wait_recv()
        return jnp.sum(gain_slots[slot : slot + size], axis=0)

    for half in range(2):

        @pl.when(role == half)
        def _():
            landed(grad_in.at[others], GRAD, half)

    def flip(matrix):
        return matrix.astype(jnp.float32).T.astype(jnp.bfloat16)

    def finish(half, block):
        place = pl.ds(pl.multiple_of(half * HALF + block * BLOCK, BLOCK), BLOCK)
        start = pl.multiple_of(block * PER_BLOCK, PER_BLOCK)
        for index in range(2):
            out_box[1 + index, half, pl.ds(start, PER_BLOCK)] = (
                sums[index, :, place].T.astype(jnp.bfloat16).reshape(PER_BLOCK, CHUNK, HEAD)
            )

    def backward_step(turn, carry):
        step = jnp.where(role == 0, STEPS - 1 - turn, turn)
        start = pl.multiple_of(step * PER_BLOCK, PER_BLOCK)
        grad = grad_in[pl.ds(start, PER_BLOCK)].reshape(BLOCK, HEAD)
        grad_flipped = flip(grad)
        q_flipped = flip(rows_of(0, role, step))
        dq = jnp.zeros((BLOCK, HEAD), jnp.float32)
        for part in range(PARTS):
            half, block = key_block(step, part)
            place = pl.ds(pl.multiple_of(half * HALF + block * BLOCK, BLOCK), BLOCK)
            grad_weights = contract(grad, rows_of(2, half, block), 1, 1)
            grad_scores = (grad_weights * slopes[step, part]).astype(jnp.bfloat16)
            sums[0, :, place] += contract(q_flipped, grad_scores, 1, 0)
            sums[1, :, place] += contract(grad_flipped, weights[step, part], 1, 0)
            dq = dq + contract(grad_scores, rows_of(1, half, block), 1, 0)
        out_box[0, role, pl.ds(start, PER_BLOCK)] = dq.astype(jnp.bfloat16).reshape(
            PER_BLOCK, CHUNK, HEAD
        )
        finish(role, step)

        def send(shard, here):
            for half in range(2):

                @pl.when(role == half)
                def _():
                    back = back_early if half == 0 else back_late.at[:, 1]
                    src, dst = out_box.at[:, half, shard], back.at[:, :, columns(head)]
                    if here:
                        dst[...] = src[...]
                    else:
                        push(src, dst, BACK, half, shard)

        each_owner(step, send)
        return carry

    lax.fori_loop(0, STEPS, backward_step, 0)

    @pl.when(role == 1)
    def _():
        def finish_early(block, carry):
            finish(0, block)

            def send(shard, here):
                src, dst = out_box.at[1:, 0, shard], back_late.at[1:, 0, :, columns(head)]
                if here:
                    dst[...] = src[...]
                else:
                    push(src, dst, BACK_E, 0, shard)

            each_owner(block, send)
            return carry

        lax.fori_loop(0, STEPS, finish_early, 0)

    landed(gain_slots.at[others], GAIN, 0)
    total = jnp.sum(gain_slots[:PEERS], axis=0)
    for stage in range(len(stages)):
        gain_send(stage, total)
        total = gain_stage_sum(stage)
    gain_total[...] = total

    def wait_back(half, count):
        cols = slice(0, count * HEAD)
        if half == 0:
            landed(back_early.at[:, :, cols], BACK, 0)
        else:
            landed(back_late.at[:, 1, :, cols], BACK, 1)
            landed(back_late.at[1:, 0, :, cols], BACK_E, 0)

    by_role(wait_back)
    grad_queries[0] = back_early[0]
    grad_queries[1] = back_late[0, 1]
    for index, result in ((1, grad_keys), (2, grad_values)):
        result[0] = (
            back_early[index].astype(jnp.float32) + back_late[index, 0].astype(jnp.float32)
        ).astype(jnp.bfloat16)
        result[1] = back_late[index, 1]

    if STAGGER:

        @pl.when(core == 1)
        def _():
            inputs_left()

    else:
        inputs_left()
    for half in range(2):

        @pl.when(role == half)
        def _():
            left(att_out.at[others], ATT, half)
            left(out_box.at[:, 0, others], BACK, half)
            if half == 1:
                left(out_box.at[1:, 0, others], BACK_E, 0)

    by_role(lambda half, count: left(grad_in.at[:count], GRAD, half))
    left(gain_slots.at[others], GAIN, 0)
    for stage, (slot, _, size) in enumerate(stages):
        gain_copy(gain_slots.at[slot : slot + size - 1], stage, group).wait_send()


def hand_over(*refs):
    count = (len(refs) - 1) // 2
    copies = [
        pltpu.make_async_copy(src, dst, refs[-1].at[index])
        for index, (src, dst) in enumerate(zip(refs[:count], refs[count : 2 * count]))
    ]
    for copy in copies:
        copy.start()
    for copy in copies:
        copy.wait()


def body(queries, key_vectors, value_vectors, gate_values, cotangent, norm_gain, lengths):
    row_count, width = queries.shape
    groups = lax.axis_size("dp")
    _, slots = gain_stages(groups)
    halves = (2, CHUNK, width)
    wide = jax.ShapeDtypeStruct(halves, jnp.bfloat16)
    vmem = pl.BlockSpec(memory_space=pltpu.VMEM)
    hbm = pl.BlockSpec(memory_space=pltpu.HBM)

    def kernel(*refs):
        attention_kernel(groups, *refs)

    shapes = (wide, wide, wide, wide, jax.ShapeDtypeStruct((HEADS, HEAD), jnp.float32))
    results = pl.pallas_call(
        kernel,
        out_shape=shapes,
        in_specs=[hbm] * 7,
        out_specs=(vmem,) * 5,
        scratch_shapes=[
            pltpu.SMEM(lengths.shape, jnp.int32),
            pltpu.VMEM((3,) + halves, jnp.bfloat16),
            pltpu.VMEM(halves, jnp.bfloat16),
            pltpu.VMEM(halves, jnp.bfloat16),
            pltpu.VMEM((1, width), jnp.float32),
            pltpu.VMEM((3, 2, PEERS, CHUNK, HEAD), jnp.bfloat16),
            pltpu.VMEM((STEPS, PARTS, BLOCK, BLOCK), jnp.bfloat16),
            pltpu.VMEM((STEPS, PARTS, BLOCK, BLOCK), jnp.float32),
            pltpu.VMEM((PEERS, CHUNK, HEAD), jnp.bfloat16),
            pltpu.VMEM(halves, jnp.bfloat16),
            pltpu.VMEM(halves, jnp.bfloat16),
            pltpu.VMEM((PEERS, CHUNK, HEAD), jnp.bfloat16),
            pltpu.VMEM((2, HEAD, 2 * HALF), jnp.float32),
            pltpu.VMEM((3, 2, PEERS, CHUNK, HEAD), jnp.bfloat16),
            pltpu.VMEM((3, CHUNK, width), jnp.bfloat16),
            pltpu.VMEM((3, 2, CHUNK, width), jnp.bfloat16),
            pltpu.VMEM((slots, HEADS, HEAD), jnp.float32),
            pltpu.SemaphoreType.DMA((7,)),
            pltpu.SemaphoreType.DMA((KINDS, 2)),
            pltpu.SemaphoreType.DMA((KINDS, 2)),
            pltpu.SemaphoreType.DMA((8,)),
            pltpu.SemaphoreType.DMA((8,)),
            pltpu.SemaphoreType.REGULAR,
        ],
        compiler_params=pltpu.CompilerParams(
            collective_id=0, has_side_effects=True, vmem_limit_bytes=60 * 2**20
        ),
    )(
        lengths,
        *(
            array.reshape(halves)
            for array in (queries, key_vectors, value_vectors, gate_values, cotangent)
        ),
        norm_gain.reshape(1, width),
    )
    *grads, gain_total = pl.pallas_call(
        hand_over,
        out_shape=shapes,
        in_specs=[vmem] * 5,
        out_specs=(hbm,) * 5,
        scratch_shapes=[pltpu.SemaphoreType.DMA((5,))],
    )(*results)
    return *(array.reshape(row_count, width) for array in grads), gain_total.reshape(width)


def solution(mesh):
    rows = P(("dp", "ctx"), None)
    return jax.shard_map(
        body,
        mesh=mesh,
        in_specs=(rows,) * 5 + (P(), P("dp", None)),
        out_specs=(rows,) * 4 + (P(),),
        check_vma=False,
    )
```

time: 476 us -> 73.3 us (0.15)
  waiting for transfers between devices: 148 us -> 0 us
  blocking collectives: 102 us -> 0 us
  matrix products: 94 us -> 0 us
  Pallas kernels: 0 us -> 72.2 us
  local copies, waits for them, and re-layouts: 51.9 us -> 0 us
  other arithmetic: 37.2 us -> 0 us
  loops' own time: 23.7 us -> 0 us
  between operations: 14.6 us -> 0.64 us
    all_gather x4 -> x0, waiting for transfers between devices: 148 us -> none  [the longest x1 76 us: body(): lax.all_gather(value_vectors, 'ctx', axis=0, tiled=True)]
    psum x1 -> x0, blocking collectives: 102 us -> none  [body(): grad_gain = lax.psum(jnp.sum(normed * grads * gates, axis=0), ('dp', 'ctx'))]
    dot_general x51 -> x0, matrix products: 94 us -> none  [the longest x17 27.4 us: head_scores(): jnp.einsum('rhd,chd->hrc', head_split(left), head_split(right), preferred...]
    pallas_call x0 -> x2, Pallas kernels: none -> 72.2 us  [the longest x1 70 us: body(): pl.pallas_call(kernel, out_shape=shapes, in_specs=[hbm] * 7, out_specs=(v...]
    dynamic_slice x32 -> x0, local copies, waits for them, and re-layouts: 34.7 us -> none  [fold_step(): lax.dynamic_slice_in_dim(array, offset, row_count, 0)]
    reduce_or x33 -> x0, other arithmetic: 24.9 us -> none  [the longest x16 11.8 us: query_fold(): return lax.cond(jnp.any(live > 0.0), query_work, keep_carry, running)]
    another operation x35 -> x0, loops' own time: 23.7 us -> none  [the longest x2 22.1 us: fold_shards(): return lax.fori_loop(0, shard_count, fold_step, initial)]
    another operation x1 -> x0, local copies, waits for them, and re-layouts: 6.5 us -> none
  transfers between devices with their start and end apart: 4 -> 0, of which waited for: 2 -> 0; matrix products, arithmetic and copies ran while one was open for 31% -> 0% of each run, Pallas kernels for 0% -> 0%
where the time goes in v2:
time: 73.3 us; the launch traced here: 72.9 us
  Pallas kernels  72.2 us (98%)
    pallas_call x1, Pallas kernels, body(): pl.pallas_call(kernel, out_shape=shapes, in_specs=[hbm] * 7, out_specs=(v...  70 us
    pallas_call x1, Pallas kernels, body(): pl.pallas_call(hand_over, out_shape=shapes, in_specs=[vmem] * 5, out_spec...  2.2 us

profile of v2, /device:TPU:6, one launch (start us, length us, event | category | flops | bytes accessed | tf_op | source)
XLA Modules:
  0.0 72.9 jit_solution(7782884700366274219)
XLA Ops:
  0.6 70.0 %shard_map.110 = (bf16[2,64,1024]{2,1,0:T(8,128)(2,1)}, bf16[2,64,1024]{2,1,0:T(8,128)(2,1)}, bf16[2,64,1024]{2,1,0:T(8,128)(2,1)}, bf16[2,64,1024]{2,1,0:T(8,128)(2,1)}, f32[8,128]{1,0:T(8,128)}) custom-call(s32[1,4]{1,0:T(1,128)} %refs_0_.1, bf16[2,64,1024]{2,1,0:T(8,128)(2,1)} %bitcast.11, bf16[2,64,1024]{2,1,0:T(8,128)(2,1)} %bitcast.12, ...), custom_call_target="tpu_custom_call" | custom-call | tf_op jit(solution)/shard_map/pallas_call | solution.py:551
  70.7 2.2 %shard_map.111 = (bf16[2,64,1024]{2,1,0:T(8,128)(2,1)}, bf16[2,64,1024]{2,1,0:T(8,128)(2,1)}, bf16[2,64,1024]{2,1,0:T(8,128)(2,1)}, bf16[2,64,1024]{2,1,0:T(8,128)(2,1)}, f32[8,128]{1,0:T(8,128)}) custom-call(bf16[2,64,1024]{2,1,0:T(8,128)(2,1)} %get-tuple-element.15.refs_0_, bf16[2,64,1024]{2,1,0:T(8,128)(2,1)} %get-tuple-element.16.refs_1_, ...), custom_call_target="tpu_custom_call" | custom-call | tf_op jit(solution)/shard_map/pallas_call | solution.py:592

commit v3 on v2

--- a/solution.py
+++ b/solution.py
@@ -18,10 +18,9 @@
 STEPS = HALF // BLOCK
 PARTS = STEPS + 1
 SCALE = 1.0 / math.sqrt(HEAD)
-STAGGER = True
-
-QUERY, KEY, VALUE, ATT, GRAD, BACK, BACK_E, GAIN = range(8)
-KINDS = 8
+
+QUERY, KEY, VALUE, ATT, GRAD, BACK, BACK_E, GAIN, GAIN_CORE, GAIN_LAYER = range(10)
+KINDS = 10
 MESH = pl.DeviceIdType.MESH
 
 
@@ -29,15 +28,6 @@
     return lax.dot_general(
         left, right, (((left_axis,), (right_axis,)), ((), ())), preferred_element_type=jnp.float32
     )
-
-
-def gain_stages(groups):
-    stages, stride, slot = [], 1, PEERS
-    while stride < groups:
-        size = min(4, groups // stride)
-        stages.append((slot, stride, size))
-        slot, stride = slot + size, stride * size
-    return stages, slot
 
 
 def attention_kernel(
@@ -74,16 +64,15 @@
     local_sem,
     send_sem,
     recv_sem,
-    gain_send_sem,
-    gain_recv_sem,
-    go_sem,
+    word_sem,
 ):
     me = lax.axis_index("ctx")
     group = lax.axis_index("dp")
     core = group % 2
     head = me // 2
     role = (me + core) % 2
-    stages, _ = gain_stages(groups)
+    place_z, layers = group // 2, groups // 2
+    partner = group + 1 - 2 * core
 
     staged = [
         pltpu.make_async_copy(src, dst, local_sem.at[index])
@@ -127,29 +116,21 @@
     def worker(which, kind_role):
         return 2 * which + (kind_role + core) % 2
 
-    def stage_peer(stride, size, turn):
-        place = group // stride % size
-        return group + ((place + turn) % size - place) * stride
+    def layer(distance):
+        return 2 * lax.rem(place_z + distance + layers, layers) + core
 
     barrier = pltpu.get_barrier_semaphore()
     for turn in range(1, PEERS):
         pl.semaphore_signal(
             barrier, inc=1, device_id={"ctx": lax.rem(me + turn, PEERS)}, device_id_type=MESH
         )
-    greeted = PEERS - 1
-    for _, stride, size in stages:
-        for turn in range(1, size):
-            pl.semaphore_signal(
-                barrier,
-                inc=1,
-                device_id={"dp": stage_peer(stride, size, turn)},
-                device_id_type=MESH,
-            )
-            greeted += 1
+    neighbours = [partner] + ([layer(1), layer(-1)] if layers > 1 else [])
+    for peer in neighbours:
+        pl.semaphore_signal(barrier, inc=1, device_id={"dp": peer}, device_id_type=MESH)
     sums[...] = jnp.zeros(sums.shape, jnp.float32)
     for copy in staged[:4]:
         copy.wait()
-    pl.semaphore_wait(barrier, greeted)
+    pl.semaphore_wait(barrier, PEERS - 1 + len(neighbours))
 
     @pl.when(role == 0)
     def _():
@@ -160,12 +141,18 @@
         box[0, 1, me] = own[0, 1, :, columns(head)]
         box[1:, :, me] = own[1:, :, :, columns(head)]
 
-    partner = group + 1 - 2 * core
-    if STAGGER:
-
-        @pl.when(core == 1)
-        def _():
-            pl.semaphore_wait(go_sem, 1)
+    rounds = [1 << index for index in range(8) if 1 << index < layers // 2 + layers % 2]
+
+    def pass_word(index):
+        if index < len(rounds):
+            for distance in (rounds[index], -rounds[index]):
+                pl.semaphore_signal(
+                    word_sem.at[index], inc=1, device_id={"dp": layer(distance)}, device_id_type=MESH
+                )
+
+    def hear_word(index):
+        if index < len(rounds):
+            pl.semaphore_wait(word_sem.at[index], 2)
 
     def each_worker(work):
         def step(turn, carry):
@@ -224,12 +211,7 @@
 
         by_role(wait)
 
-    if STAGGER:
-
-        @pl.when(core == 0)
-        def _():
-            inputs_left()
-            pl.semaphore_signal(go_sem, inc=1, device_id={"dp": partner}, device_id_type=MESH)
+    pass_word(0)
 
     ends = []
     total = 0
@@ -288,6 +270,8 @@
         return carry
 
     lax.fori_loop(0, STEPS, score_step, 0)
+    hear_word(0)
+    pass_word(1)
 
     @pl.when(role == 0)
     def _():
@@ -337,6 +321,8 @@
         return carry
 
     lax.fori_loop(0, STEPS, attend_step, 0)
+    hear_word(1)
+    pass_word(2)
     for copy in staged[4:]:
         copy.wait()
     gain_row = gain[...]
@@ -374,12 +360,14 @@
         )
     )
 
-    def gain_copy(slot, stage, target):
+    both, along = PEERS, PEERS + 2
+
+    def gain_copy(slots, kind, target):
         return pltpu.make_async_remote_copy(
-            src_ref=slot,
-            dst_ref=slot,
-            send_sem=gain_send_sem.at[stage],
-            recv_sem=gain_recv_sem.at[stage],
+            src_ref=slots,
+            dst_ref=slots,
+            send_sem=send_sem.at[kind, 0],
+            recv_sem=recv_sem.at[kind, 0],
             device_id={"dp": target},
             device_id_type=MESH,
         )
@@ -393,18 +381,23 @@
 
     lax.fori_loop(1, PEERS, send_gain, 0)
 
-    def gain_send(stage, total):
-        slot, stride, size = stages[stage]
-        mine = slot + group // stride % size
-        gain_slots[mine] = total
-        for turn in range(1, size):
-            gain_copy(gain_slots.at[mine], stage, stage_peer(stride, size, turn)).start()
-
-    def gain_stage_sum(stage):
-        slot, stride, size = stages[stage]
-        gain_copy(gain_slots.at[slot : slot + size - 1], stage, group).wait_recv()
-        return jnp.sum(gain_slots[slot : slot + size], axis=0)
-
+    def gain_over_cores():
+        landed(gain_slots.at[others], GAIN, 0)
+        gain_slots[both + core] = jnp.sum(gain_slots[:PEERS], axis=0)
+        gain_copy(gain_slots.at[both + core], GAIN_CORE, partner).start()
+
+    def gain_over_layers():
+        gain_copy(gain_slots.at[both], GAIN_CORE, partner).wait_recv()
+        mine = along + place_z
+        gain_slots[mine] = gain_slots[both] + gain_slots[both + 1]
+
+        def send(distance, carry):
+            gain_copy(gain_slots.at[mine], GAIN_LAYER, layer(distance)).start()
+            return carry
+
+        lax.fori_loop(1, layers, send, 0)
+
+    hear_word(2)
     for half in range(2):
 
         @pl.when(role == half)
@@ -422,7 +415,10 @@
                 sums[index, :, place].T.astype(jnp.bfloat16).reshape(PER_BLOCK, CHUNK, HEAD)
             )
 
+    gain_over_cores()
+
     def backward_step(turn, carry):
+        pl.when(turn == 2)(gain_over_layers)
         step = jnp.where(role == 0, STEPS - 1 - turn, turn)
         start = pl.multiple_of(step * PER_BLOCK, PER_BLOCK)
         grad = grad_in[pl.ds(start, PER_BLOCK)].reshape(BLOCK, HEAD)
@@ -476,13 +472,6 @@
 
         lax.fori_loop(0, STEPS, finish_early, 0)
 
-    landed(gain_slots.at[others], GAIN, 0)
-    total = jnp.sum(gain_slots[:PEERS], axis=0)
-    for stage in range(len(stages)):
-        gain_send(stage, total)
-        total = gain_stage_sum(stage)
-    gain_total[...] = total
-
     def wait_back(half, count):
         cols = slice(0, count * HEAD)
         if half == 0:
@@ -492,6 +481,9 @@
             landed(back_late.at[1:, 0, :, cols], BACK_E, 0)
 
     by_role(wait_back)
+    if layers > 1:
+        gain_copy(gain_slots.at[along : along + layers - 1], GAIN_LAYER, partner).wait_recv()
+    gain_total[...] = jnp.sum(gain_slots[along : along + layers], axis=0)
     grad_queries[0] = back_early[0]
     grad_queries[1] = back_late[0, 1]
     for index, result in ((1, grad_keys), (2, grad_values)):
@@ -500,14 +492,7 @@
         ).astype(jnp.bfloat16)
         result[1] = back_late[index, 1]
 
-    if STAGGER:
-
-        @pl.when(core == 1)
-        def _():
-            inputs_left()
-
-    else:
-        inputs_left()
+    inputs_left()
     for half in range(2):
 
         @pl.when(role == half)
@@ -519,8 +504,9 @@
 
     by_role(lambda half, count: left(grad_in.at[:count], GRAD, half))
     left(gain_slots.at[others], GAIN, 0)
-    for stage, (slot, _, size) in enumerate(stages):
-        gain_copy(gain_slots.at[slot : slot + size - 1], stage, group).wait_send()
+    gain_copy(gain_slots.at[both], GAIN_CORE, partner).wait_send()
+    if layers > 1:
+        gain_copy(gain_slots.at[along : along + layers - 1], GAIN_LAYER, partner).wait_send()
 
 
 def hand_over(*refs):
@@ -538,7 +524,6 @@
 def body(queries, key_vectors, value_vectors, gate_values, cotangent, norm_gain, lengths):
     row_count, width = queries.shape
     groups = lax.axis_size("dp")
-    _, slots = gain_stages(groups)
     halves = (2, CHUNK, width)
     wide = jax.ShapeDtypeStruct(halves, jnp.bfloat16)
     vmem = pl.BlockSpec(memory_space=pltpu.VMEM)
@@ -570,13 +555,11 @@
             pltpu.VMEM((3, 2, PEERS, CHUNK, HEAD), jnp.bfloat16),
             pltpu.VMEM((3, CHUNK, width), jnp.bfloat16),
             pltpu.VMEM((3, 2, CHUNK, width), jnp.bfloat16),
-            pltpu.VMEM((slots, HEADS, HEAD), jnp.float32),
+            pltpu.VMEM((PEERS + 2 + groups // 2, HEADS, HEAD), jnp.float32),
             pltpu.SemaphoreType.DMA((7,)),
             pltpu.SemaphoreType.DMA((KINDS, 2)),
             pltpu.SemaphoreType.DMA((KINDS, 2)),
-            pltpu.SemaphoreType.DMA((8,)),
-            pltpu.SemaphoreType.DMA((8,)),
-            pltpu.SemaphoreType.REGULAR,
+            pltpu.SemaphoreType.REGULAR((8,)),
         ],
         compiler_params=pltpu.CompilerParams(
             collective_id=0, has_side_effects=True, vmem_limit_bytes=60 * 2**20

time: 73.3 us -> 64 us (0.87)
  the two profiles are of different devices: /device:TPU:6 before, /device:TPU:26 now
where the time goes in v3:
time: 64 us; the launch traced here: 63.8 us
  Pallas kernels  63.2 us (99%)
  between operations  0.64 us (1%)
    pallas_call x1, Pallas kernels, body(): pl.pallas_call(kernel, out_shape=shapes, in_specs=[hbm] * 7, out_specs=(v...  61 us
    pallas_call x1, Pallas kernels, body(): pl.pallas_call(hand_over, out_shape=shapes, in_specs=[vmem] * 5, out_spec...  2.2 us

profile of v3, /device:TPU:26, one launch (start us, length us, event | category | flops | bytes accessed | tf_op | source)
XLA Modules:
  0.0 63.8 jit_solution(9267683137403464115)
XLA Ops:
  0.6 61.0 %shard_map.110 = (bf16[2,64,1024]{2,1,0:T(8,128)(2,1)}, bf16[2,64,1024]{2,1,0:T(8,128)(2,1)}, bf16[2,64,1024]{2,1,0:T(8,128)(2,1)}, bf16[2,64,1024]{2,1,0:T(8,128)(2,1)}, f32[8,128]{1,0:T(8,128)}) custom-call(s32[1,4]{1,0:T(1,128)} %refs_0_.1, bf16[2,64,1024]{2,1,0:T(8,128)(2,1)} %bitcast.11, bf16[2,64,1024]{2,1,0:T(8,128)(2,1)} %bitcast.12, ...), custom_call_target="tpu_custom_call" | custom-call | tf_op jit(solution)/shard_map/pallas_call | solution.py:536
  61.7 2.2 %shard_map.111 = (bf16[2,64,1024]{2,1,0:T(8,128)(2,1)}, bf16[2,64,1024]{2,1,0:T(8,128)(2,1)}, bf16[2,64,1024]{2,1,0:T(8,128)(2,1)}, bf16[2,64,1024]{2,1,0:T(8,128)(2,1)}, f32[8,128]{1,0:T(8,128)}) custom-call(bf16[2,64,1024]{2,1,0:T(8,128)(2,1)} %get-tuple-element.15.refs_0_, bf16[2,64,1024]{2,1,0:T(8,128)(2,1)} %get-tuple-element.16.refs_1_, ...), custom_call_target="tpu_custom_call" | custom-call | tf_op jit(solution)/shard_map/pallas_call | solution.py:575

commit v4 on v3

v4 whole, which is shorter than its diff:
```python
import math

import jax
import jax.numpy as jnp
from jax import lax
from jax.experimental import pallas as pl
from jax.experimental.pallas import tpu as pltpu
from jax.sharding import PartitionSpec as P

HEAD = 128
EPSILON = 1e-05
PEERS = 16
HEADS = 8
CHUNK = 64
HALF = PEERS * CHUNK
BLOCK = 256
PER_BLOCK = BLOCK // CHUNK
BLOCKS = HALF // BLOCK
PARTS = BLOCKS + 1
EARLY_STEPS = BLOCKS // 2
STEPS = EARLY_STEPS + BLOCKS
SCALE = 1.0 / math.sqrt(HEAD)

QUERY_KEY, VALUE, ATT, GRAD, DQ, DKV, GAIN, GAIN_CORE, GAIN_LAYER, GAIN_TOTAL = range(10)
KINDS = 10
MESH = pl.DeviceIdType.MESH


def contract(left, right, left_axis, right_axis):
    return lax.dot_general(
        left, right, (((left_axis,), (right_axis,)), ((), ())), preferred_element_type=jnp.float32
    )


def attention_kernel(
    groups,
    lengths_hbm,
    queries_hbm,
    keys_hbm,
    values_hbm,
    gates_hbm,
    cotangent_hbm,
    gain_hbm,
    output_hbm,
    grad_queries_hbm,
    grad_keys_hbm,
    grad_values_hbm,
    gain_total_hbm,
    lengths,
    own,
    gates,
    cotangent,
    gain,
    box,
    bounds,
    weights,
    slopes,
    att_sum,
    att_out,
    att_in,
    output,
    grad_out,
    grad_in,
    q_flipped,
    grad_flipped,
    dq_sum,
    sums,
    out_box,
    back,
    gain_slots,
    gain_total,
    local_sem,
    out_sem,
    send_sem,
    recv_sem,
    word_sem,
):
    me = lax.axis_index("ctx")
    group = lax.axis_index("dp")
    core = group % 2
    head = me // 2
    works = me % 2 == core
    place_z, layers = group // 2, groups // 2
    mate = me + 1 - 2 * (me % 2)
    partner = group + 1 - 2 * core
    others = slice(0, PEERS - 1)

    staged = [
        pltpu.make_async_copy(src, dst, local_sem.at[index])
        for index, (src, dst) in enumerate(
            (
                (queries_hbm, own.at[0]),
                (keys_hbm, own.at[1]),
                (values_hbm, own.at[2]),
                (lengths_hbm, lengths),
                (gates_hbm, gates),
                (cotangent_hbm, cotangent),
                (gain_hbm, gain),
            )
        )
    ]
    for copy in staged:
        copy.start()

    def columns(which):
        return pl.ds(pl.multiple_of(which * HEAD, HEAD), HEAD)

    def remote(src, dst, kind, half, target):
        return pltpu.make_async_remote_copy(
            src_ref=src,
            dst_ref=dst,
            send_sem=send_sem.at[kind, half],
            recv_sem=recv_sem.at[kind, half],
            device_id={"ctx": target},
            device_id_type=MESH,
        )

    def push(src, dst, kind, half, target):
        remote(src, dst, kind, half, target).start()

    def landed(ref, kind, half=0):
        remote(ref, ref, kind, half, me).wait_recv()

    def left(ref, kind, half=0):
        remote(ref, ref, kind, half, me).wait_send()

    def layer(distance):
        return 2 * lax.rem(place_z + distance + layers, layers) + core

    barrier = pltpu.get_barrier_semaphore()
    for turn in range(1, PEERS):
        pl.semaphore_signal(
            barrier, inc=1, device_id={"ctx": lax.rem(me + turn, PEERS)}, device_id_type=MESH
        )
    near = [{"dp": partner, "ctx": mate}]
    if layers > 1:
        near += [{"dp": layer(1)}, {"dp": layer(-1)}]

    @pl.when(jnp.logical_not(works))
    def _():
        for peer in near:
            pl.semaphore_signal(barrier, inc=1, device_id=peer, device_id_type=MESH)

    for copy in staged[:4]:
        copy.wait()

    @pl.when(works)
    def _():
        pl.semaphore_wait(barrier, PEERS - 1)

    @pl.when(jnp.logical_not(works))
    def _():
        pl.semaphore_wait(barrier, PEERS - 1 + len(near))

    rounds = [1 << index for index in range(8) if 1 << index < layers // 2 + layers % 2]

    def pass_words():
        for index, reach in enumerate(rounds):
            for distance in (reach, -reach):
                pl.semaphore_signal(
                    word_sem.at[index], inc=1, device_id={"dp": layer(distance)}, device_id_type=MESH
                )
            pl.semaphore_wait(word_sem.at[index], 2)

    def each_worker(work):
        def step(turn, carry):
            which = lax.rem(head + turn, HEADS)
            work(which, 2 * which + core)
            return carry

        lax.fori_loop(jnp.where(works, 1, 0), HEADS, step, 0)

    def by_count(work):
        @pl.when(works)
        def _():
            work(HEADS - 1)

        @pl.when(jnp.logical_not(works))
        def _():
            work(HEADS)

    each_worker(
        lambda which, peer: push(
            own.at[:2, :, :, columns(which)], box.at[:2, :, me], QUERY_KEY, 0, peer
        )
    )

    @pl.when(works)
    def _():
        box[:, :, me] = own[:, :, :, columns(head)]

    by_count(lambda count: left(box.at[:2, :, :count], QUERY_KEY))
    each_worker(
        lambda which, peer: push(own.at[2, :, :, columns(which)], box.at[2, :, me], VALUE, 0, peer)
    )
    pl.when(jnp.logical_not(works))(pass_words)

    def times(half, block, shape, axis):
        place = lax.broadcasted_iota(jnp.int32, shape, axis)
        chunk, inner = place // CHUNK, place % CHUNK
        shard = block * PER_BLOCK + chunk
        return jnp.where(half == 0, shard, 2 * PEERS - 1 - shard) * CHUNK + inner

    def rows_of(which, half, block):
        start = pl.multiple_of(block * PER_BLOCK, PER_BLOCK)
        return box[which, half, pl.ds(start, PER_BLOCK)].reshape(BLOCK, HEAD)

    def chunks(block):
        return pl.ds(pl.multiple_of(block * PER_BLOCK, PER_BLOCK), PER_BLOCK)

    def place_of(half, block):
        return pl.ds(pl.multiple_of(half * HALF + block * BLOCK, BLOCK), BLOCK)

    def pair(step, part):
        early = step < EARLY_STEPS
        short = part <= step
        late_block = step - EARLY_STEPS
        reaches_back = part <= late_block
        q_half = jnp.where(early, 0, 1)
        q_block = jnp.where(early, jnp.where(short, step, BLOCKS - 1 - step), late_block)
        k_half = jnp.where(early | reaches_back, 0, 1)
        k_block = jnp.where(
            early,
            jnp.where(short, part, part - step - 1),
            jnp.where(reaches_back, BLOCKS - 1 - late_block + part, part - 1),
        )
        return q_half, q_block, k_half, k_block

    def for_blocks(step, work):
        @pl.when(step < EARLY_STEPS)
        def _():
            work(0, step)
            work(0, BLOCKS - 1 - step)

        @pl.when(step >= EARLY_STEPS)
        def _():
            work(1, step - EARLY_STEPS)

    def each_owner(block, work):
        for part in range(PER_BLOCK):
            shard = block * PER_BLOCK + part

            @pl.when(shard != me)
            def _():
                work(shard, False)

            @pl.when(shard == me)
            def _():
                work(shard, True)

    def deliver(src, dst, kind, half, shard, here):
        if here:
            dst[...] = src[...]
        else:
            push(src, dst, kind, half, shard)

    @pl.when(works)
    def _():
        ends = []
        total = 0
        for user in range(lengths.shape[1]):
            total = total + lengths[0, user]
            ends.append(total)

        def bounds_step(index, carry):
            half, block = index // BLOCKS, index % BLOCKS
            q_time = times(half, block, (BLOCK, HEAD), 0)
            first = jnp.zeros((BLOCK, HEAD), jnp.int32)
            for end in ends:
                first = jnp.where(q_time >= end, end, first)
            bounds[0, half, block] = first
            bounds[1, half, block] = q_time
            return carry

        lax.fori_loop(0, 2 * BLOCKS, bounds_step, 0)
        sums[...] = jnp.zeros(sums.shape, jnp.float32)
        dq_sum[...] = jnp.zeros(dq_sum.shape, jnp.float32)
        att_sum[...] = jnp.zeros(att_sum.shape, jnp.float32)
        landed(box.at[:2, :, others], QUERY_KEY)

        def score_step(step, carry):
            for part in range(PARTS):
                q_half, q_block, k_half, k_block = pair(step, part)
                k_time = times(k_half, k_block, (1, BLOCK), 1)
                first = jnp.tile(bounds[0, q_half, q_block], (1, BLOCK // HEAD))
                q_time = jnp.tile(bounds[1, q_half, q_block], (1, BLOCK // HEAD))
                raw = contract(rows_of(0, q_half, q_block), rows_of(1, k_half, k_block), 1, 1)
                scores = raw * SCALE
                live = (k_time >= first) & (k_time <= q_time)
                sigmoid = 0.5 * jnp.tanh(raw * (0.5 * SCALE)) + 0.5
                silu = scores * sigmoid
                slope = sigmoid * SCALE + silu * (SCALE - SCALE * sigmoid)
                weights[step, part] = jnp.where(live, silu, 0.0).astype(jnp.bfloat16)
                slopes[step, part] = jnp.where(live, slope, 0.0)
            return carry

        lax.fori_loop(0, STEPS, score_step, 0)

    @pl.when(works)
    def _():
        landed(box.at[2, :, others], VALUE)

        def attend_step(step, carry):
            for part in range(PARTS):
                q_half, q_block, k_half, k_block = pair(step, part)
                att_sum[place_of(q_half, q_block), :] += contract(
                    weights[step, part], rows_of(2, k_half, k_block), 1, 0
                )

            def send(half, block):
                att_out[half, chunks(block)] = (
                    att_sum[place_of(half, block), :]
                    .astype(jnp.bfloat16)
                    .reshape(PER_BLOCK, CHUNK, HEAD)
                )
                each_owner(
                    block,
                    lambda shard, here: deliver(
                        att_out.at[half, shard],
                        att_in.at[half, :, columns(head)],
                        ATT,
                        half,
                        shard,
                        here,
                    ),
                )

            for_blocks(step, send)
            return carry

        lax.fori_loop(0, STEPS, attend_step, 0)

    def flip(matrix):
        return matrix.astype(jnp.float32).T.astype(jnp.bfloat16)

    @pl.when(works)
    def _():
        def flip_step(block, carry):
            for half in range(2):
                q_flipped[half, block] = flip(rows_of(0, half, block))
            return carry

        lax.fori_loop(0, BLOCKS, flip_step, 0)

    for copy in staged[4:]:
        copy.wait()
    gain_row = gain[...]

    def normalize_half(half):
        by_count(lambda count: landed(att_in.at[half, :, : count * HEAD], ATT, half))

        def normalize(part, gain_sum):
            rows = pl.ds(pl.multiple_of(part * 32, 32), 32)
            attended = att_in[half, rows, :].astype(jnp.float32)
            centered = attended - jnp.mean(attended, axis=1, keepdims=True)
            variance = jnp.mean(centered * centered, axis=1, keepdims=True)
            inverse = lax.rsqrt(variance + EPSILON)
            normed = centered * inverse
            gate = gates[half, rows, :].astype(jnp.float32)
            grad = cotangent[half, rows, :].astype(jnp.float32)
            scaled = gate * gain_row
            output[half, rows, :] = (normed * scaled).astype(jnp.bfloat16)
            gain_sum = gain_sum + jnp.sum(normed * grad * gate, axis=0, keepdims=True)
            grad = grad * scaled
            grad_out[half, rows, :] = (
                (
                    grad
                    - jnp.mean(grad, axis=1, keepdims=True)
                    - normed * jnp.mean(grad * normed, axis=1, keepdims=True)
                )
                * inverse
            ).astype(jnp.bfloat16)
            return gain_sum

        gain_sum = lax.fori_loop(
            0, CHUNK // 32, normalize, jnp.zeros((1, gain.shape[1]), jnp.float32)
        )
        each_worker(
            lambda which, peer: push(
                grad_out.at[half, :, columns(which)], grad_in.at[half, me], GRAD, half, peer
            )
        )

        @pl.when(works)
        def _():
            grad_in[half, me] = grad_out[half, :, columns(head)]

        return gain_sum

    gain_sum = normalize_half(0)
    gain_sum = gain_sum + normalize_half(1)
    output_copy = pltpu.make_async_copy(output, output_hbm, out_sem.at[0])
    output_copy.start()

    both, along = PEERS, PEERS + 2

    def gain_copy(slots, kind, target):
        return pltpu.make_async_remote_copy(
            src_ref=slots,
            dst_ref=slots,
            send_sem=send_sem.at[kind, 0],
            recv_sem=recv_sem.at[kind, 0],
            device_id=target,
            device_id_type=MESH,
        )

    for which in range(HEADS):
        gain_slots[me, which : which + 1, :] = gain_sum[:, which * HEAD : (which + 1) * HEAD]

    def send_gain(turn, carry):
        adder = 2 * lax.rem(head + turn, HEADS) + 1 - core
        push(gain_slots.at[me], gain_slots.at[me], GAIN, 0, adder)
        return carry

    lax.fori_loop(jnp.where(works, 0, 1), HEADS, send_gain, 0)

    def gain_over_groups():
        landed(gain_slots.at[others], GAIN)
        gain_slots[both + core] = jnp.sum(gain_slots[:PEERS], axis=0)
        gain_copy(gain_slots.at[both + core], GAIN_CORE, near[0]).start()
        gain_copy(gain_slots.at[both], GAIN_CORE, near[0]).wait_recv()
        mine = along + place_z
        gain_slots[mine] = gain_slots[both] + gain_slots[both + 1]

        def send(distance, carry):
            gain_copy(gain_slots.at[mine], GAIN_LAYER, {"dp": layer(distance)}).start()
            return carry

        if layers > 1:
            lax.fori_loop(1, layers, send, 0)
            gain_copy(gain_slots.at[along : along + layers - 1], GAIN_LAYER, near[0]).wait_recv()
        gain_total[...] = jnp.sum(gain_slots[along : along + layers], axis=0)
        push(gain_total, gain_total, GAIN_TOTAL, 0, mate)

    def finish(half, block):
        for index in range(2):
            out_box[1 + index, half, chunks(block)] = (
                sums[index, :, place_of(half, block)]
                .T.astype(jnp.bfloat16)
                .reshape(PER_BLOCK, CHUNK, HEAD)
            )

    def backward_step(step, carry):
        def prepare(half, block):
            grad_flipped[half, block] = flip(grad_in[half, chunks(block)].reshape(BLOCK, HEAD))

        for_blocks(step, prepare)
        for part in range(PARTS):
            q_half, q_block, k_half, k_block = pair(step, part)
            grad = grad_in[q_half, chunks(q_block)].reshape(BLOCK, HEAD)
            place = place_of(k_half, k_block)
            grad_weights = contract(grad, rows_of(2, k_half, k_block), 1, 1)
            grad_scores = (grad_weights * slopes[step, part]).astype(jnp.bfloat16)
            sums[0, :, place] += contract(q_flipped[q_half, q_block], grad_scores, 1, 0)
            sums[1, :, place] += contract(grad_flipped[q_half, q_block], weights[step, part], 1, 0)
            dq_sum[place_of(q_half, q_block), :] += contract(
                grad_scores, rows_of(1, k_half, k_block), 1, 0
            )

        def send_queries(half, block):
            out_box[0, half, chunks(block)] = (
                dq_sum[place_of(half, block), :]
                .astype(jnp.bfloat16)
                .reshape(PER_BLOCK, CHUNK, HEAD)
            )
            if half == 1:
                finish(1, block)
            count = 1 + 2 * half
            each_owner(
                block,
                lambda shard, here: deliver(
                    out_box.at[:count, half, shard],
                    back.at[:count, half, :, columns(head)],
                    DQ,
                    half,
                    shard,
                    here,
                ),
            )

        for_blocks(step, send_queries)
        return carry

    pl.when(jnp.logical_not(works))(gain_over_groups)

    @pl.when(works)
    def _():
        landed(grad_in.at[0, others], GRAD, 0)

        def wait_and_step(step, carry):
            @pl.when(step == EARLY_STEPS)
            def _():
                landed(grad_in.at[1, others], GRAD, 1)

            return backward_step(step, carry)

        lax.fori_loop(0, STEPS, wait_and_step, 0)

        def finish_early(block, carry):
            finish(0, block)
            each_owner(
                block,
                lambda shard, here: deliver(
                    out_box.at[1:, 0, shard],
                    back.at[1:, 0, :, columns(head)],
                    DKV,
                    0,
                    shard,
                    here,
                ),
            )
            return carry

        lax.fori_loop(0, BLOCKS, finish_early, 0)

    def wait_back(count):
        cols = slice(0, count * HEAD)
        landed(back.at[0, 0, :, cols], DQ, 0)
        landed(back.at[:, 1, :, cols], DQ, 1)
        landed(back.at[1:, 0, :, cols], DKV)

    by_count(wait_back)
    results = [
        pltpu.make_async_copy(back.at[index], result, out_sem.at[1 + index])
        for index, result in enumerate((grad_queries_hbm, grad_keys_hbm, grad_values_hbm))
    ]
    for copy in results:
        copy.start()
    pl.when(works)(lambda: landed(gain_total, GAIN_TOTAL))
    results.append(pltpu.make_async_copy(gain_total, gain_total_hbm, out_sem.at[4]))
    results[-1].start()

    @pl.when(works)
    def _():
        for half in range(2):
            left(att_out.at[half, others], ATT, half)
        left(out_box.at[0, 0, others], DQ, 0)
        left(out_box.at[:, 1, others], DQ, 1)
        left(out_box.at[1:, 0, others], DKV)

    def inputs_left(count):
        left(box.at[2, :, :count], VALUE)
        for half in range(2):
            left(grad_in.at[half, :count], GRAD, half)

    by_count(inputs_left)

    @pl.when(works)
    def _():
        left(gain_slots.at[:HEADS], GAIN)

    @pl.when(jnp.logical_not(works))
    def _():
        left(gain_slots.at[: HEADS - 1], GAIN)
        gain_copy(gain_slots.at[both], GAIN_CORE, near[0]).wait_send()
        if layers > 1:
            gain_copy(gain_slots.at[along : along + layers - 1], GAIN_LAYER, near[0]).wait_send()
        left(gain_total, GAIN_TOTAL)

    output_copy.wait()
    for copy in results:
        copy.wait()


def hand_over(*refs):
    count = (len(refs) - 1) // 2
    copies = [
        pltpu.make_async_copy(src, dst, refs[-1].at[index])
        for index, (src, dst) in enumerate(zip(refs[:count], refs[count : 2 * count]))
    ]
    for copy in copies:
        copy.start()
    for copy in copies:
        copy.wait()


def body(queries, key_vectors, value_vectors, gate_values, cotangent, norm_gain, lengths):
    row_count, width = queries.shape
    groups = lax.axis_size("dp")
    halves = (2, CHUNK, width)
    wide = jax.ShapeDtypeStruct(halves, jnp.bfloat16)
    vmem = pl.BlockSpec(memory_space=pltpu.VMEM)
    hbm = pl.BlockSpec(memory_space=pltpu.HBM)
    boxes = (2, PEERS, CHUNK, HEAD)

    def kernel(*refs):
        attention_kernel(groups, *refs)

    shapes = (wide, wide, wide, wide, jax.ShapeDtypeStruct((HEADS, HEAD), jnp.float32))
    results = pl.pallas_call(
        kernel,
        out_shape=shapes,
        in_specs=[hbm] * 7,
        out_specs=(hbm,) * 5,
        scratch_shapes=[
            pltpu.SMEM(lengths.shape, jnp.int32),
            pltpu.VMEM((3,) + halves, jnp.bfloat16),
            pltpu.VMEM(halves, jnp.bfloat16),
            pltpu.VMEM(halves, jnp.bfloat16),
            pltpu.VMEM((1, width), jnp.float32),
            pltpu.VMEM((3,) + boxes, jnp.bfloat16),
            pltpu.VMEM((2, 2, BLOCKS, BLOCK, HEAD), jnp.int32),
            pltpu.VMEM((STEPS, PARTS, BLOCK, BLOCK), jnp.bfloat16),
            pltpu.VMEM((STEPS, PARTS, BLOCK, BLOCK), jnp.float32),
            pltpu.VMEM((2 * HALF, HEAD), jnp.float32),
            pltpu.VMEM(boxes, jnp.bfloat16),
            pltpu.VMEM(halves, jnp.bfloat16),
            pltpu.VMEM(halves, jnp.bfloat16),
            pltpu.VMEM(halves, jnp.bfloat16),
            pltpu.VMEM(boxes, jnp.bfloat16),
            pltpu.VMEM((2, BLOCKS, HEAD, BLOCK), jnp.bfloat16),
            pltpu.VMEM((2, BLOCKS, HEAD, BLOCK), jnp.bfloat16),
            pltpu.VMEM((2 * HALF, HEAD), jnp.float32),
            pltpu.VMEM((2, HEAD, 2 * HALF), jnp.float32),
            pltpu.VMEM((3,) + boxes, jnp.bfloat16),
            pltpu.VMEM((3,) + halves, jnp.bfloat16),
            pltpu.VMEM((PEERS + 2 + groups // 2, HEADS, HEAD), jnp.float32),
            pltpu.VMEM((HEADS, HEAD), jnp.float32),
            pltpu.SemaphoreType.DMA((7,)),
            pltpu.SemaphoreType.DMA((5,)),
            pltpu.SemaphoreType.DMA((KINDS, 2)),
            pltpu.SemaphoreType.DMA((KINDS, 2)),
            pltpu.SemaphoreType.REGULAR((8,)),
        ],
        compiler_params=pltpu.CompilerParams(
            collective_id=0, has_side_effects=True, vmem_limit_bytes=60 * 2**20
        ),
    )(
        lengths,
        *(
            array.reshape(halves)
            for array in (queries, key_vectors, value_vectors, gate_values, cotangent)
        ),
        norm_gain.reshape(1, width),
    )
    *grads, gain_total = pl.pallas_call(
        hand_over,
        out_shape=shapes,
        in_specs=[vmem] * 5,
        out_specs=(hbm,) * 5,
        scratch_shapes=[pltpu.SemaphoreType.DMA((5,))],
    )(*results)
    return *(array.reshape(row_count, width) for array in grads), gain_total.reshape(width)


def solution(mesh):
    rows = P(("dp", "ctx"), None)
    return jax.shard_map(
        body,
        mesh=mesh,
        in_specs=(rows,) * 5 + (P(), P("dp", None)),
        out_specs=(rows,) * 4 + (P(),),
        check_vma=False,
    )
```

time: 64 us -> 59.1 us (0.923)
  the two profiles are of different devices: /device:TPU:26 before, /device:TPU:6 now
where the time goes in v4:
time: 59.1 us; the launch traced here: 58.9 us
  Pallas kernels  58.2 us (98%)
  between operations  0.64 us (1%)
    pallas_call x1, Pallas kernels, body(): pl.pallas_call(kernel, out_shape=shapes, in_specs=[hbm] * 7, out_specs=(h...  56 us
    pallas_call x1, Pallas kernels, body(): pl.pallas_call(hand_over, out_shape=shapes, in_specs=[vmem] * 5, out_spec...  2.2 us

profile of v4, /device:TPU:6, one launch (start us, length us, event | category | flops | bytes accessed | tf_op | source)
XLA Modules:
  0.0 58.9 jit_solution(14998854251678866030)
XLA Ops:
  0.6 56.0 %shard_map.110 = (bf16[2,64,1024]{2,1,0:T(8,128)(2,1)}, bf16[2,64,1024]{2,1,0:T(8,128)(2,1)}, bf16[2,64,1024]{2,1,0:T(8,128)(2,1)}, bf16[2,64,1024]{2,1,0:T(8,128)(2,1)}, f32[8,128]{1,0:T(8,128)}) custom-call(s32[1,4]{1,0:T(1,128)} %refs_0_.1, bf16[2,64,1024]{2,1,0:T(8,128)(2,1)} %bitcast.11, bf16[2,64,1024]{2,1,0:T(8,128)(2,1)} %bitcast.12, ...), custom_call_target="tpu_custom_call" | custom-call | tf_op jit(solution)/shard_map/pallas_call | solution.py:590
  56.7 2.2 %shard_map.111 = (bf16[2,64,1024]{2,1,0:T(8,128)(2,1)}, bf16[2,64,1024]{2,1,0:T(8,128)(2,1)}, bf16[2,64,1024]{2,1,0:T(8,128)(2,1)}, bf16[2,64,1024]{2,1,0:T(8,128)(2,1)}, f32[8,128]{1,0:T(8,128)}) custom-call(bf16[2,64,1024]{2,1,0:T(8,128)(2,1)} %get-tuple-element.15.refs_0_, bf16[2,64,1024]{2,1,0:T(8,128)(2,1)} %get-tuple-element.16.refs_1_, ...), custom_call_target="tpu_custom_call" | custom-call | tf_op jit(solution)/shard_map/pallas_call | solution.py:636

commit v5 on v4

--- a/solution.py
+++ b/solution.py
@@ -17,12 +17,14 @@
 PER_BLOCK = BLOCK // CHUNK
 BLOCKS = HALF // BLOCK
 PARTS = BLOCKS + 1
+ROW = 4
+ROWS_OF_PEERS = PEERS // ROW
 EARLY_STEPS = BLOCKS // 2
 STEPS = EARLY_STEPS + BLOCKS
 SCALE = 1.0 / math.sqrt(HEAD)
 
-QUERY_KEY, VALUE, ATT, GRAD, DQ, DKV, GAIN, GAIN_CORE, GAIN_LAYER, GAIN_TOTAL = range(10)
-KINDS = 10
+QUERY_KEY, VALUE, ATT, GRAD, DQ, DKV, GAIN, GAIN_LAYER, GAIN_TOTAL = range(9)
+KINDS = 9
 MESH = pl.DeviceIdType.MESH
 
 
@@ -73,6 +75,7 @@
     out_sem,
     send_sem,
     recv_sem,
+    grad_sem,
     word_sem,
 ):
     me = lax.axis_index("ctx")
@@ -81,7 +84,8 @@
     head = me // 2
     works = me % 2 == core
     place_z, layers = group // 2, groups // 2
-    mate = me + 1 - 2 * (me % 2)
+    row, adder_place = me // ROW, 1 + core
+    adds = me % ROW == adder_place
     partner = group + 1 - 2 * core
     others = slice(0, PEERS - 1)
 
@@ -132,11 +136,11 @@
         pl.semaphore_signal(
             barrier, inc=1, device_id={"ctx": lax.rem(me + turn, PEERS)}, device_id_type=MESH
         )
-    near = [{"dp": partner, "ctx": mate}]
+    near = [{"dp": partner, "ctx": row * ROW + 2 - core}]
     if layers > 1:
         near += [{"dp": layer(1)}, {"dp": layer(-1)}]
 
-    @pl.when(jnp.logical_not(works))
+    @pl.when(adds)
     def _():
         for peer in near:
             pl.semaphore_signal(barrier, inc=1, device_id=peer, device_id_type=MESH)
@@ -144,17 +148,28 @@
     for copy in staged[:4]:
         copy.wait()
 
-    @pl.when(works)
+    @pl.when(jnp.logical_not(adds))
     def _():
         pl.semaphore_wait(barrier, PEERS - 1)
 
-    @pl.when(jnp.logical_not(works))
+    @pl.when(adds)
     def _():
         pl.semaphore_wait(barrier, PEERS - 1 + len(near))
 
     rounds = [1 << index for index in range(8) if 1 << index < layers // 2 + layers % 2]
 
+    def row_mates(work):
+        for turn in range(1, ROW):
+            work(row * ROW + (me + turn) % ROW)
+
     def pass_words():
+        pl.semaphore_signal(word_sem.at[6], inc=1, device_id=near[0], device_id_type=MESH)
+        pl.semaphore_wait(word_sem.at[6], 1)
+        row_mates(
+            lambda peer: pl.semaphore_signal(
+                word_sem.at[7], inc=1, device_id={"ctx": peer}, device_id_type=MESH
+            )
+        )
         for index, reach in enumerate(rounds):
             for distance in (reach, -reach):
                 pl.semaphore_signal(
@@ -179,21 +194,26 @@
         def _():
             work(HEADS)
 
-    each_worker(
-        lambda which, peer: push(
-            own.at[:2, :, :, columns(which)], box.at[:2, :, me], QUERY_KEY, 0, peer
-        )
-    )
+    for half in range(2):
+        each_worker(
+            lambda which, peer: push(
+                own.at[:2, half, :, columns(which)], box.at[:2, half, me], QUERY_KEY, half, peer
+            )
+        )
 
     @pl.when(works)
     def _():
         box[:, :, me] = own[:, :, :, columns(head)]
 
-    by_count(lambda count: left(box.at[:2, :, :count], QUERY_KEY))
+    def queries_keys_left(count):
+        for half in range(2):
+            left(box.at[:2, half, :count], QUERY_KEY, half)
+
+    by_count(queries_keys_left)
     each_worker(
         lambda which, peer: push(own.at[2, :, :, columns(which)], box.at[2, :, me], VALUE, 0, peer)
     )
-    pl.when(jnp.logical_not(works))(pass_words)
+    pl.when(adds)(pass_words)
 
     def times(half, block, shape, axis):
         place = lax.broadcasted_iota(jnp.int32, shape, axis)
@@ -276,7 +296,7 @@
         sums[...] = jnp.zeros(sums.shape, jnp.float32)
         dq_sum[...] = jnp.zeros(dq_sum.shape, jnp.float32)
         att_sum[...] = jnp.zeros(att_sum.shape, jnp.float32)
-        landed(box.at[:2, :, others], QUERY_KEY)
+        landed(box.at[:2, 0, others], QUERY_KEY, 0)
 
         def score_step(step, carry):
             for part in range(PARTS):
@@ -294,7 +314,9 @@
                 slopes[step, part] = jnp.where(live, slope, 0.0)
             return carry
 
-        lax.fori_loop(0, STEPS, score_step, 0)
+        lax.fori_loop(0, EARLY_STEPS, score_step, 0)
+        landed(box.at[:2, 1, others], QUERY_KEY, 1)
+        lax.fori_loop(EARLY_STEPS, STEPS, score_step, 0)
 
     @pl.when(works)
     def _():
@@ -346,7 +368,73 @@
         copy.wait()
     gain_row = gain[...]
 
-    def normalize_half(half):
+    def grad_copy(src, dst, half, block, target):
+        return pltpu.make_async_remote_copy(
+            src_ref=src,
+            dst_ref=dst,
+            send_sem=send_sem.at[GRAD, half],
+            recv_sem=grad_sem.at[half, block],
+            device_id={"ctx": target},
+            device_id_type=MESH,
+        )
+
+    def grads_landed(half, block):
+        @pl.when(me // PER_BLOCK == block)
+        def _():
+            rest = grad_in.at[half, : PER_BLOCK - 1]
+            grad_copy(rest, rest, half, block, me).wait_recv()
+
+        @pl.when(me // PER_BLOCK != block)
+        def _():
+            rest = grad_in.at[half, :PER_BLOCK]
+            grad_copy(rest, rest, half, block, me).wait_recv()
+
+    along = 2 * PEERS
+
+    def gain_copy(slots, kind, target):
+        return pltpu.make_async_remote_copy(
+            src_ref=slots,
+            dst_ref=slots,
+            send_sem=send_sem.at[kind, 0],
+            recv_sem=recv_sem.at[kind, 0],
+            device_id=target,
+            device_id_type=MESH,
+        )
+
+    def send_gain(gain_sum):
+        mine = core * PEERS + me
+        for which in range(HEADS):
+            gain_slots[mine, which : which + 1, :] = gain_sum[:, which * HEAD : (which + 1) * HEAD]
+        pl.when(jnp.logical_not(adds))(lambda: pl.semaphore_wait(word_sem.at[7], 1))
+        for turn in range(ROWS_OF_PEERS):
+            start = (row + turn) % ROWS_OF_PEERS * ROW
+            if turn == 0:
+
+                @pl.when(jnp.logical_not(adds))
+                def _():
+                    gain_copy(gain_slots.at[mine], GAIN, {"ctx": start + adder_place}).start()
+
+            else:
+                gain_copy(gain_slots.at[mine], GAIN, {"ctx": start + adder_place}).start()
+            other = {"dp": partner, "ctx": start + 2 - core}
+            gain_copy(gain_slots.at[mine], GAIN, other).start()
+
+    def gain_over_groups():
+        gain_copy(gain_slots.at[: 2 * PEERS - 1], GAIN, near[0]).wait_recv()
+        mine = along + place_z
+        gain_slots[mine] = jnp.sum(gain_slots[: 2 * PEERS], axis=0)
+
+        def send(distance, carry):
+            gain_copy(gain_slots.at[mine], GAIN_LAYER, {"dp": layer(distance)}).start()
+            return carry
+
+        if layers > 1:
+            lax.fori_loop(1, layers, send, 0)
+            gain_copy(gain_slots.at[along : along + layers - 1], GAIN_LAYER, near[0]).wait_recv()
+        gain_total[...] = jnp.sum(gain_slots[along : along + layers], axis=0)
+        row_mates(lambda peer: push(gain_total, gain_total, GAIN_TOTAL, 0, peer))
+
+    def normalize_half(half, gain_before):
         by_count(lambda count: landed(att_in.at[half, :, : count * HEAD], ATT, half))
 
         def normalize(part, gain_sum):
@@ -373,12 +461,14 @@
             return gain_sum
 
         gain_sum = lax.fori_loop(
-            0, CHUNK // 32, normalize, jnp.zeros((1, gain.shape[1]), jnp.float32)
-        )
+            0, CHUNK // 32, normalize, gain_before
+        )
+        if half == 1:
+            send_gain(gain_sum)
         each_worker(
-            lambda which, peer: push(
-                grad_out.at[half, :, columns(which)], grad_in.at[half, me], GRAD, half, peer
-            )
+            lambda which, peer: grad_copy(
+                grad_out.at[half, :, columns(which)], grad_in.at[half, me], half, me // PER_BLOCK, peer
+            ).start()
         )
 
         @pl.when(works)
@@ -387,50 +477,9 @@
 
         return gain_sum
 
-    gain_sum = normalize_half(0)
-    gain_sum = gain_sum + normalize_half(1)
+    normalize_half(1, normalize_half(0, jnp.zeros((1, gain.shape[1]), jnp.float32)))
     output_copy = pltpu.make_async_copy(output, output_hbm, out_sem.at[0])
     output_copy.start()
-
-    both, along = PEERS, PEERS + 2
-
-    def gain_copy(slots, kind, target):
-        return pltpu.make_async_remote_copy(
-            src_ref=slots,
-            dst_ref=slots,
-            send_sem=send_sem.at[kind, 0],
-            recv_sem=recv_sem.at[kind, 0],
-            device_id=target,
-            device_id_type=MESH,
-        )
-
-    for which in range(HEADS):
-        gain_slots[me, which : which + 1, :] = gain_sum[:, which * HEAD : (which + 1) * HEAD]
-
-    def send_gain(turn, carry):
-        adder = 2 * lax.rem(head + turn, HEADS) + 1 - core
-        push(gain_slots.at[me], gain_slots.at[me], GAIN, 0, adder)
-        return carry
-
-    lax.fori_loop(jnp.where(works, 0, 1), HEADS, send_gain, 0)
-
-    def gain_over_groups():
-        landed(gain_slots.at[others], GAIN)
-        gain_slots[both + core] = jnp.sum(gain_slots[:PEERS], axis=0)
-        gain_copy(gain_slots.at[both + core], GAIN_CORE, near[0]).start()
-        gain_copy(gain_slots.at[both], GAIN_CORE, near[0]).wait_recv()
-        mine = along + place_z
-        gain_slots[mine] = gain_slots[both] + gain_slots[both + 1]
-
-        def send(distance, carry):
-            gain_copy(gain_slots.at[mine], GAIN_LAYER, {"dp": layer(distance)}).start()
-            return carry
-
-        if layers > 1:
-            lax.fori_loop(1, layers, send, 0)
-            gain_copy(gain_slots.at[along : along + layers - 1], GAIN_LAYER, near[0]).wait_recv()
-        gain_total[...] = jnp.sum(gain_slots[along : along + layers], axis=0)
-        push(gain_total, gain_total, GAIN_TOTAL, 0, mate)
 
     def finish(half, block):
         for index in range(2):
@@ -442,6 +491,7 @@
 
     def backward_step(step, carry):
         def prepare(half, block):
+            grads_landed(half, block)
             grad_flipped[half, block] = flip(grad_in[half, chunks(block)].reshape(BLOCK, HEAD))
 
         for_blocks(step, prepare)
@@ -481,20 +531,11 @@
         for_blocks(step, send_queries)
         return carry
 
-    pl.when(jnp.logical_not(works))(gain_over_groups)
+    pl.when(adds)(gain_over_groups)
 
     @pl.when(works)
     def _():
-        landed(grad_in.at[0, others], GRAD, 0)
-
-        def wait_and_step(step, carry):
-            @pl.when(step == EARLY_STEPS)
-            def _():
-                landed(grad_in.at[1, others], GRAD, 1)
-
-            return backward_step(step, carry)
-
-        lax.fori_loop(0, STEPS, wait_and_step, 0)
+        lax.fori_loop(0, STEPS, backward_step, 0)
 
         def finish_early(block, carry):
             finish(0, block)
@@ -526,7 +567,7 @@
     ]
     for copy in results:
         copy.start()
-    pl.when(works)(lambda: landed(gain_total, GAIN_TOTAL))
+    pl.when(jnp.logical_not(adds))(lambda: landed(gain_total, GAIN_TOTAL))
     results.append(pltpu.make_async_copy(gain_total, gain_total_hbm, out_sem.at[4]))
     results[-1].start()
 
@@ -545,17 +586,16 @@
 
     by_count(inputs_left)
 
-    @pl.when(works)
-    def _():
-        left(gain_slots.at[:HEADS], GAIN)
-
-    @pl.when(jnp.logical_not(works))
-    def _():
-        left(gain_slots.at[: HEADS - 1], GAIN)
-        gain_copy(gain_slots.at[both], GAIN_CORE, near[0]).wait_send()
+    @pl.when(jnp.logical_not(adds))
+    def _():
+        left(gain_slots.at[: 2 * ROWS_OF_PEERS], GAIN)
+
+    @pl.when(adds)
+    def _():
+        left(gain_slots.at[: 2 * ROWS_OF_PEERS - 1], GAIN)
         if layers > 1:
             gain_copy(gain_slots.at[along : along + layers - 1], GAIN_LAYER, near[0]).wait_send()
-        left(gain_total, GAIN_TOTAL)
+        left(gain_slots.at[: ROW - 1], GAIN_TOTAL)
 
     output_copy.wait()
     for copy in results:
@@ -563,14 +603,22 @@
 
 
 def hand_over(*refs):
-    count = (len(refs) - 1) // 2
-    copies = [
+    count = (len(refs) - 2) // 3
+    sources, results, held = refs[:count], refs[count : 2 * count], refs[2 * count : 3 * count]
+    into = [
+        pltpu.make_async_copy(src, dst, refs[-2].at[index])
+        for index, (src, dst) in enumerate(zip(sources, held))
+    ]
+    out = [
         pltpu.make_async_copy(src, dst, refs[-1].at[index])
-        for index, (src, dst) in enumerate(zip(refs[:count], refs[count : 2 * count]))
+        for index, (src, dst) in enumerate(zip(held, results))
     ]
-    for copy in copies:
+    for copy in into:
         copy.start()
-    for copy in copies:
+    for copy, after in zip(into, out):
+        copy.wait()
+        after.start()
+    for copy in out:
         copy.wait()
 
 
@@ -579,7 +627,6 @@
     groups = lax.axis_size("dp")
     halves = (2, CHUNK, width)
     wide = jax.ShapeDtypeStruct(halves, jnp.bfloat16)
-    vmem = pl.BlockSpec(memory_space=pltpu.VMEM)
     hbm = pl.BlockSpec(memory_space=pltpu.HBM)
     boxes = (2, PEERS, CHUNK, HEAD)
 
@@ -614,12 +661,13 @@
             pltpu.VMEM((2, HEAD, 2 * HALF), jnp.float32),
             pltpu.VMEM((3,) + boxes, jnp.bfloat16),
             pltpu.VMEM((3,) + halves, jnp.bfloat16),
-            pltpu.VMEM((PEERS + 2 + groups // 2, HEADS, HEAD), jnp.float32),
+            pltpu.VMEM((2 * PEERS + groups // 2, HEADS, HEAD), jnp.float32),
             pltpu.VMEM((HEADS, HEAD), jnp.float32),
             pltpu.SemaphoreType.DMA((7,)),
             pltpu.SemaphoreType.DMA((5,)),
             pltpu.SemaphoreType.DMA((KINDS, 2)),
             pltpu.SemaphoreType.DMA((KINDS, 2)),
+            pltpu.SemaphoreType.DMA((2, BLOCKS)),
             pltpu.SemaphoreType.REGULAR((8,)),
         ],
         compiler_params=pltpu.CompilerParams(
@@ -636,9 +684,11 @@
     *grads, gain_total = pl.pallas_call(
         hand_over,
         out_shape=shapes,
-        in_specs=[vmem] * 5,
+        in_specs=[hbm] * 5,
         out_specs=(hbm,) * 5,
-        scratch_shapes=[pltpu.SemaphoreType.DMA((5,))],
+        scratch_shapes=[pltpu.VMEM(shape.shape, shape.dtype) for shape in shapes]
+        + [pltpu.SemaphoreType.DMA((5,))] * 2,
+        compiler_params=pltpu.CompilerParams(vmem_limit_bytes=60 * 2**20),
     )(*results)
     return *(array.reshape(row_count, width) for array in grads), gain_total.reshape(width)
 

time: 59.1 us -> 57.4 us (0.971)
  Pallas kernels: 58.2 us -> 56.6 us
    pallas_call x1, Pallas kernels: 56 us -> 54.6 us  [body(): pl.pallas_call(kernel, out_shape=shapes, in_specs=[hbm] * 7, out_specs=(h...]
where the time goes in v5:
time: 57.4 us; the launch traced here: 57.3 us
  Pallas kernels  56.6 us (99%)
  between operations  0.64 us (1%)
    pallas_call x1, Pallas kernels, body(): pl.pallas_call(kernel, out_shape=shapes, in_specs=[hbm] * 7, out_specs=(h...  54.6 us
    pallas_call x1, Pallas kernels, body(): pl.pallas_call(hand_over, out_shape=shapes, in_specs=[hbm] * 5, out_specs...  2 us

profile of v5, /device:TPU:6, one launch (start us, length us, event | category | flops | bytes accessed | tf_op | source)
XLA Modules:
  0.0 57.3 jit_solution(6286319530388915199)
XLA Ops:
  0.6 54.6 %shard_map.110 = (bf16[2,64,1024]{2,1,0:T(8,128)(2,1)}, bf16[2,64,1024]{2,1,0:T(8,128)(2,1)}, bf16[2,64,1024]{2,1,0:T(8,128)(2,1)}, bf16[2,64,1024]{2,1,0:T(8,128)(2,1)}, f32[8,128]{1,0:T(8,128)}) custom-call(s32[1,4]{1,0:T(1,128)} %refs_0_.1, bf16[2,64,1024]{2,1,0:T(8,128)(2,1)} %bitcast.11, bf16[2,64,1024]{2,1,0:T(8,128)(2,1)} %bitcast.12, ...), custom_call_target="tpu_custom_call" | custom-call | tf_op jit(solution)/shard_map/pallas_call | solution.py:637
  55.3 2.0 %shard_map.111 = (bf16[2,64,1024]{2,1,0:T(8,128)(2,1)}, bf16[2,64,1024]{2,1,0:T(8,128)(2,1)}, bf16[2,64,1024]{2,1,0:T(8,128)(2,1)}, bf16[2,64,1024]{2,1,0:T(8,128)(2,1)}, f32[8,128]{1,0:T(8,128)}) custom-call(bf16[2,64,1024]{2,1,0:T(8,128)(2,1)} %get-tuple-element.15.refs_0_, bf16[2,64,1024]{2,1,0:T(8,128)(2,1)} %get-tuple-element.16.refs_1_, ...), custom_call_target="tpu_custom_call" | custom-call | tf_op jit(solution)/shard_map/pallas_call | solution.py:684

commit v6 on v5

--- a/solution.py
+++ b/solution.py
@@ -353,7 +353,7 @@
         lax.fori_loop(0, STEPS, attend_step, 0)
 
     def flip(matrix):
-        return matrix.astype(jnp.float32).T.astype(jnp.bfloat16)
+        return matrix.T
 
     @pl.when(works)
     def _():
@@ -485,7 +485,8 @@
         for index in range(2):
             out_box[1 + index, half, chunks(block)] = (
                 sums[index, :, place_of(half, block)]
-                .T.astype(jnp.bfloat16)
+                .astype(jnp.bfloat16)
+                .T
                 .reshape(PER_BLOCK, CHUNK, HEAD)
             )
 
@@ -495,17 +496,39 @@
             grad_flipped[half, block] = flip(grad_in[half, chunks(block)].reshape(BLOCK, HEAD))
 
         for_blocks(step, prepare)
-        for part in range(PARTS):
-            q_half, q_block, k_half, k_block = pair(step, part)
-            grad = grad_in[q_half, chunks(q_block)].reshape(BLOCK, HEAD)
-            place = place_of(k_half, k_block)
-            grad_weights = contract(grad, rows_of(2, k_half, k_block), 1, 1)
-            grad_scores = (grad_weights * slopes[step, part]).astype(jnp.bfloat16)
-            sums[0, :, place] += contract(q_flipped[q_half, q_block], grad_scores, 1, 0)
-            sums[1, :, place] += contract(grad_flipped[q_half, q_block], weights[step, part], 1, 0)
-            dq_sum[place_of(q_half, q_block), :] += contract(
-                grad_scores, rows_of(1, k_half, k_block), 1, 0
-            )
+        @pl.when(step < EARLY_STEPS)
+        def _():
+            for part in range(PARTS):
+                q_half, q_block, k_half, k_block = pair(step, part)
+                grad = grad_in[q_half, chunks(q_block)].reshape(BLOCK, HEAD)
+                place = place_of(k_half, k_block)
+                grad_weights = contract(grad, rows_of(2, k_half, k_block), 1, 1)
+                grad_scores = (grad_weights * slopes[step, part]).astype(jnp.bfloat16)
+                sums[0, :, place] += contract(q_flipped[q_half, q_block], grad_scores, 1, 0)
+                sums[1, :, place] += contract(grad_flipped[q_half, q_block], weights[step, part], 1, 0)
+                dq_sum[place_of(q_half, q_block), :] += contract(
+                    grad_scores, rows_of(1, k_half, k_block), 1, 0
+                )
+
+        @pl.when(step >= EARLY_STEPS)
+        def _():
+            q_block = step - EARLY_STEPS
+            grad = grad_in[1, chunks(q_block)].reshape(BLOCK, HEAD)
+            met = [pair(step, part)[2:] for part in range(PARTS)]
+            window = [
+                jnp.concatenate([rows_of(which, *each) for each in met], axis=0) for which in (1, 2)
+            ]
+            grad_weights = contract(grad, window[1], 1, 1)
+            slope = jnp.concatenate([slopes[step, part] for part in range(PARTS)], axis=1)
+            weight = jnp.concatenate([weights[step, part] for part in range(PARTS)], axis=1)
+            grad_scores = (grad_weights * slope).astype(jnp.bfloat16)
+            dq_sum[place_of(1, q_block), :] = contract(grad_scores, window[0], 1, 0)
+            dk = contract(q_flipped[1, q_block], grad_scores, 1, 0)
+            dv = contract(grad_flipped[1, q_block], weight, 1, 0)
+            for part, each in enumerate(met):
+                cols = slice(part * BLOCK, (part + 1) * BLOCK)
+                sums[0, :, place_of(*each)] += dk[:, cols]
+                sums[1, :, place_of(*each)] += dv[:, cols]
 
         def send_queries(half, block):
             out_box[0, half, chunks(block)] = (
@@ -554,21 +577,22 @@
 
         lax.fori_loop(0, BLOCKS, finish_early, 0)
 
-    def wait_back(count):
-        cols = slice(0, count * HEAD)
-        landed(back.at[0, 0, :, cols], DQ, 0)
-        landed(back.at[:, 1, :, cols], DQ, 1)
-        landed(back.at[1:, 0, :, cols], DKV)
-
-    by_count(wait_back)
-    results = [
-        pltpu.make_async_copy(back.at[index], result, out_sem.at[1 + index])
-        for index, result in enumerate((grad_queries_hbm, grad_keys_hbm, grad_values_hbm))
-    ]
-    for copy in results:
+    def result_copy(index, half, slot):
+        result = (grad_queries_hbm, grad_keys_hbm, grad_values_hbm)[index]
+        return pltpu.make_async_copy(back.at[index, half], result.at[half], out_sem.at[slot])
+
+    results = [result_copy(0, 0, 1), result_copy(0, 1, 2), result_copy(1, 1, 3), result_copy(2, 1, 4)]
+    by_count(lambda count: landed(back.at[0, 0, :, : count * HEAD], DQ, 0))
+    results[0].start()
+    by_count(lambda count: landed(back.at[:, 1, :, : count * HEAD], DQ, 1))
+    for copy in results[1:]:
+        copy.start()
+    by_count(lambda count: landed(back.at[1:, 0, :, : count * HEAD], DKV))
+    results += [result_copy(1, 0, 5), result_copy(2, 0, 6)]
+    for copy in results[-2:]:
         copy.start()
     pl.when(jnp.logical_not(adds))(lambda: landed(gain_total, GAIN_TOTAL))
-    results.append(pltpu.make_async_copy(gain_total, gain_total_hbm, out_sem.at[4]))
+    results.append(pltpu.make_async_copy(gain_total, gain_total_hbm, out_sem.at[7]))
     results[-1].start()
 
     @pl.when(works)
@@ -664,7 +688,7 @@
             pltpu.VMEM((2 * PEERS + groups // 2, HEADS, HEAD), jnp.float32),
             pltpu.VMEM((HEADS, HEAD), jnp.float32),
             pltpu.SemaphoreType.DMA((7,)),
-            pltpu.SemaphoreType.DMA((5,)),
+            pltpu.SemaphoreType.DMA((8,)),
             pltpu.SemaphoreType.DMA((KINDS, 2)),
             pltpu.SemaphoreType.DMA((KINDS, 2)),
             pltpu.SemaphoreType.DMA((2, BLOCKS)),

time: 57.4 us -> 56.8 us (0.990); the launches traced: 57.3 us -> 55.8 us
  Pallas kernels: 56.6 us -> 55.1 us
    pallas_call x1, Pallas kernels: 54.6 us -> 53.1 us  [body(): pl.pallas_call(kernel, out_shape=shapes, in_specs=[hbm] * 7, out_specs=(h...]
where the time goes in v6:
time: 56.8 us; the launch traced here: 55.8 us
  Pallas kernels  55.1 us (97%)
  between operations  0.64 us (1%)
    pallas_call x1, Pallas kernels, body(): pl.pallas_call(kernel, out_shape=shapes, in_specs=[hbm] * 7, out_specs=(h...  53.1 us
    pallas_call x1, Pallas kernels, body(): pl.pallas_call(hand_over, out_shape=shapes, in_specs=[hbm] * 5, out_specs...  2 us

profile of v6, /device:TPU:6, one launch (start us, length us, event | category | flops | bytes accessed | tf_op | source)
XLA Modules:
  0.0 55.8 jit_solution(3171796036976358587)
XLA Ops:
  0.6 53.1 %shard_map.110 = (bf16[2,64,1024]{2,1,0:T(8,128)(2,1)}, bf16[2,64,1024]{2,1,0:T(8,128)(2,1)}, bf16[2,64,1024]{2,1,0:T(8,128)(2,1)}, bf16[2,64,1024]{2,1,0:T(8,128)(2,1)}, f32[8,128]{1,0:T(8,128)}) custom-call(s32[1,4]{1,0:T(1,128)} %refs_0_.1, bf16[2,64,1024]{2,1,0:T(8,128)(2,1)} %bitcast.11, bf16[2,64,1024]{2,1,0:T(8,128)(2,1)} %bitcast.12, ...), custom_call_target="tpu_custom_call" | custom-call | tf_op jit(solution)/shard_map/pallas_call | solution.py:661
  53.8 2.0 %shard_map.111 = (bf16[2,64,1024]{2,1,0:T(8,128)(2,1)}, bf16[2,64,1024]{2,1,0:T(8,128)(2,1)}, bf16[2,64,1024]{2,1,0:T(8,128)(2,1)}, bf16[2,64,1024]{2,1,0:T(8,128)(2,1)}, f32[8,128]{1,0:T(8,128)}) custom-call(bf16[2,64,1024]{2,1,0:T(8,128)(2,1)} %get-tuple-element.15.refs_0_, bf16[2,64,1024]{2,1,0:T(8,128)(2,1)} %get-tuple-element.16.refs_1_, ...), custom_call_target="tpu_custom_call" | custom-call | tf_op jit(solution)/shard_map/pallas_call | solution.py:708

commit v7 on v6

--- a/solution.py
+++ b/solution.py
@@ -355,15 +355,6 @@
     def flip(matrix):
         return matrix.T
 
-    @pl.when(works)
-    def _():
-        def flip_step(block, carry):
-            for half in range(2):
-                q_flipped[half, block] = flip(rows_of(0, half, block))
-            return carry
-
-        lax.fori_loop(0, BLOCKS, flip_step, 0)
-
     for copy in staged[4:]:
         copy.wait()
     gain_row = gain[...]
@@ -477,7 +468,17 @@
 
         return gain_sum
 
-    normalize_half(1, normalize_half(0, jnp.zeros((1, gain.shape[1]), jnp.float32)))
+    gain_early = normalize_half(0, jnp.zeros((1, gain.shape[1]), jnp.float32))
+    @pl.when(works)
+    def _():
+        def flip_step(block, carry):
+            for half in range(2):
+                q_flipped[half, block] = flip(rows_of(0, half, block))
+            return carry
+
+        lax.fori_loop(0, BLOCKS, flip_step, 0)
+
+    normalize_half(1, gain_early)
     output_copy = pltpu.make_async_copy(output, output_hbm, out_sem.at[0])
     output_copy.start()
 

time: 56.8 us -> 56.8 us (level)
  no operation moved by 1% of the time
where the time goes in v7:
time: 56.8 us; the launch traced here: 55.8 us
  Pallas kernels  55.1 us (97%)
  between operations  0.64 us (1%)
    pallas_call x1, Pallas kernels, body(): pl.pallas_call(kernel, out_shape=shapes, in_specs=[hbm] * 7, out_specs=(h...  53.1 us
    pallas_call x1, Pallas kernels, body(): pl.pallas_call(hand_over, out_shape=shapes, in_specs=[hbm] * 5, out_specs...  2 us

profile of v7, /device:TPU:6, one launch (start us, length us, event | category | flops | bytes accessed | tf_op | source)
XLA Modules:
  0.0 55.8 jit_solution(11708968814775912089)
XLA Ops:
  0.6 53.1 %shard_map.110 = (bf16[2,64,1024]{2,1,0:T(8,128)(2,1)}, bf16[2,64,1024]{2,1,0:T(8,128)(2,1)}, bf16[2,64,1024]{2,1,0:T(8,128)(2,1)}, bf16[2,64,1024]{2,1,0:T(8,128)(2,1)}, f32[8,128]{1,0:T(8,128)}) custom-call(s32[1,4]{1,0:T(1,128)} %refs_0_.1, bf16[2,64,1024]{2,1,0:T(8,128)(2,1)} %bitcast.11, bf16[2,64,1024]{2,1,0:T(8,128)(2,1)} %bitcast.12, ...), custom_call_target="tpu_custom_call" | custom-call | tf_op jit(solution)/shard_map/pallas_call | solution.py:662
  53.8 2.0 %shard_map.111 = (bf16[2,64,1024]{2,1,0:T(8,128)(2,1)}, bf16[2,64,1024]{2,1,0:T(8,128)(2,1)}, bf16[2,64,1024]{2,1,0:T(8,128)(2,1)}, bf16[2,64,1024]{2,1,0:T(8,128)(2,1)}, f32[8,128]{1,0:T(8,128)}) custom-call(bf16[2,64,1024]{2,1,0:T(8,128)(2,1)} %get-tuple-element.15.refs_0_, bf16[2,64,1024]{2,1,0:T(8,128)(2,1)} %get-tuple-element.16.refs_1_, ...), custom_call_target="tpu_custom_call" | custom-call | tf_op jit(solution)/shard_map/pallas_call | solution.py:709
